TPU v7x, 256 devices: a whole 4x4x8 slice. The times are simulated.
256 devices in a mesh: visit: 8 (over y, core), tile: 32 (over x, z).
Axes of the slice: x: 4, y: 4, z: 8, core: 2. Of those that a mesh axis runs over, the one named last changes fastest.
Arguments:
- image: float32 [8, 1024, 4096], P('visit', 'tile'), may hold values from -6 to 6
- variance: float32 [8, 1024, 4096], P('visit', 'tile'), may hold values from 0.5 to 2
- row_mask: int32 [8, 1024], P('visit', 'tile'), may hold values 0 or 1
- row_shift: int32 [8], P('visit'), may hold values from 0 to 511
- basis_coef: float32 [8, 5], P('visit'), may hold values from -2.5 to 2.5
- vertical: float32 [5, 21], replicated, may hold values from -1.25 to 1.25
- horizontal: float32 [5, 21], replicated, may hold values from -1.25 to 1.25
- col_weight: float32 [8, 6, 4096], P('visit'), may hold values from -0.1 to 0.4
- col_offset: int32 [8, 4096], P('visit'), may hold values from 0 to 4090, as said below
- row_weight: float32 [8, 6, 1024], P('visit', None, 'tile'), may hold values from -0.1 to 0.4
Outputs:
- coadd: float32 [1024, 4096], P('tile')
- weight_sum: float32 [1024, 4096], P('tile')
Inputs may be any that keep to these rules, and one draw needn't show every extreme that they name: Column c of visit v reads source columns col_offset to col_offset + 5, where col_offset lies from c - 5 to c.
All inputs are finite; a program needn't handle non-finite values. No bound on the sum of `row_mask` on one device may be relied on, other than what follows from the above.
Results may differ from a plain program's by a relative error of at most 0.0038.
Values may be sent and summed in bfloat16 or wider, within the bound.
A program may use at most 64 MiB of HBM per device.

v0:
```python
import jax
import jax.numpy as jnp
from jax import lax
from jax.sharding import PartitionSpec as P


def with_halo(x, sides, width):
    for axis, dim in sides:
        peers, length = (lax.axis_size(axis), x.shape[dim])
        up = [(i, (i + 1) % peers) for i in range(peers - 1)]
        down = [(j, i) for i, j in up]
        last = lax.slice_in_dim(x, length - width, length, axis=dim)
        initial = lax.slice_in_dim(x, 0, width, axis=dim)
        before = lax.ppermute(last, axis, up)
        after = lax.ppermute(initial, axis, down)
        x = jnp.concatenate([before, x, after], axis=dim)
    return x


def passed_along(x, axis, by):
    peers = lax.axis_size(axis)
    pairs = [(i, i + by) for i in range(peers) if 0 <= i + by < peers]
    return lax.ppermute(x, axis, pairs)


def match_psf(padded, vertical, horizontal, weights, rows):
    kernel = vertical.shape[1]
    rim = kernel // 2
    columns = padded.shape[1]
    result = jnp.zeros((rows, columns), jnp.float32)
    for basis in range(vertical.shape[0]):
        row_pass = jnp.zeros((rows, columns), jnp.float32)
        for offset in range(kernel):
            row_pass = row_pass + vertical[basis, offset] * padded[offset : offset + rows]
        spread = jnp.pad(row_pass, ((0, 0), (rim, rim)))
        col_pass = jnp.zeros((rows, columns), jnp.float32)
        for offset in range(kernel):
            col_pass = col_pass + horizontal[basis, offset] * spread[:, offset : offset + columns]
        result = result + weights[basis] * col_pass
    return result


def warp_columns(matched, weights, offsets):
    columns = matched.shape[1]
    taps = weights.shape[0]
    reach = 5
    lowest = -reach
    highest = taps - 1
    margin = max(reach, taps - 1)
    widened = jnp.pad(matched, ((0, 0), (margin, margin)))
    delta = offsets - jnp.arange(columns, dtype=jnp.int32)
    result = jnp.zeros(matched.shape, jnp.float32)
    for step_shift in range(lowest, highest + 1):
        factor = jnp.zeros((columns,), jnp.float32)
        for offset in range(taps):
            factor = factor + jnp.where(delta + offset == step_shift, weights[offset], 0.0)
        shifted = widened[:, margin + step_shift : margin + step_shift + columns]
        result = result + factor[None, :] * shifted
    return result


def body(
    image,
    variance,
    row_mask,
    row_shift,
    basis_coef,
    vertical,
    horizontal,
    col_weight,
    col_offset,
    row_weight,
):
    pixels = image[0]
    rows = pixels.shape[0]
    rim = vertical.shape[1] // 2
    padded = with_halo(pixels, (("tile", 0),), rim)
    matched = match_psf(padded, vertical, horizontal, basis_coef[0], rows)
    colwarp = warp_columns(matched, col_weight[0], col_offset[0])
    ivar = row_mask[0].astype(jnp.float32)[:, None] / variance[0]
    moved = jnp.stack([colwarp, ivar]).astype(jnp.bfloat16)
    amount = row_shift[0]
    block_hops = amount // rows
    remainder = amount % rows
    current = moved
    for level in range((lax.axis_size("tile") - 1).bit_length()):
        hopped = passed_along(current, "tile", 1 << level)
        current = jnp.where(block_hops >> level & 1 == 1, hopped, current)
    previous = passed_along(current, "tile", 1)
    joined = jnp.concatenate([previous, current], axis=1)
    sky = lax.dynamic_slice_in_dim(joined, rows - remainder, rows, 1)
    framed = with_halo(sky[0], (("tile", 0),), 3)
    warped = jnp.zeros(pixels.shape, jnp.float32)
    for offset in range(row_weight.shape[1]):
        warped = warped + row_weight[0, offset][:, None] * framed[
            1 + offset : 1 + offset + rows
        ].astype(jnp.float32)
    sky_ivar = sky[1].astype(jnp.float32)
    numer = sky_ivar * warped
    total_numer, total_denom = lax.psum((numer, sky_ivar), "visit")
    return (total_numer / jnp.maximum(total_denom, 1.0), total_denom)


def solution(mesh):
    placed = (
        P("visit", "tile", None),
        P("visit", "tile", None),
        P("visit", "tile"),
        P("visit"),
        P("visit", None),
        P(),
        P(),
        P("visit", None, None),
        P("visit", None),
        P("visit", None, "tile"),
    )
    return jax.shard_map(
        body,
        mesh=mesh,
        in_specs=placed,
        out_specs=(P("tile", None), P("tile", None)),
        check_vma=False,
    )
```

profile of v0, /device:TPU:1, one launch (start us, length us, event | category | flops | bytes accessed | tf_op | source)
XLA Modules:
  0.0 402.4 jit_solution(2166449920348166267)
XLA Ops:
  7.2 1.1 slice_bitcast_fusion.2
  8.3 4.5 %collective-permute-start = (f32[10,4096]{1,0:T(8,128)S(1)}, f32[10,4096]{1,0:T(8,128)S(1)}, u32[]{:S(2)}, u32[]{:S(2)}) collective-permute-start(f32[10,4096]{1,0:T(8,128)S(1)} %get-tuple-element.28), channel_id=1, source_target_pairs={{0,1},{1,2},{2,3},{3,4},{4,5},{5,6},{6,7},{7,8},{8,9},{9,10},{10,1... | collective-permute-start | bytes 491528 | tf_op jit(solution)/shard_map/ppermute | solution.py:14
  12.9 1.3 collective-permute-start.1
  19.3 0.7 fusion.190
  20.7 0.7 fusion.193
  25.4 15.3 %multiply_add_fusion.5 = (f32[32,4096]{1,0:T(8,128)S(1)}, f32[32,4096]{1,0:T(8,128)S(1)}, f32[32,4096]{1,0:T(8,128)S(1)}, f32[32,4096]{1,0:T(8,128)S(1)}, f32[32...) fusion(f32[32,4096]{1,0:T(8,128)S(1)} %bitcast.513, ...), kind=kLoop, calls=%fused_computation.210 | loop fusion | flops 7995392 | bytes 10813524 | tf_op jit(solution)/shard_map/add | solution.py:34
  40.7 13.8 %multiply_add_fusion.4 = f32[32,4096]{1,0:T(8,128)S(1)} fusion(f32[32,4096]{1,0:T(8,128)S(1)} %get-tuple-element.22, f32[32,4096]{1,0:T(8,128)S(1)} %get-tuple-element.21, f32[32,4096]{1,0:T(8,128)S(1)} %get-tuple-element.20, f32[32,4096]{1,0:T(8,128)S(1)} %get-tuple-element.19, f32[32,4096]{1,0:T(8,128)S(1)} %get-tuple-element.18, ...), kind=kLoop, calls=%fused_computation.183 | loop fusion | flops 5636096 | bytes 10813524 | tf_op jit(solution)/shard_map/add | solution.py:34
  54.5 14.0 %multiply_add_fusion.3 = f32[32,4096]{1,0:T(8,128)S(1)} fusion(f32[32,4096]{1,0:T(8,128)S(1)} %get-tuple-element.22, f32[32,4096]{1,0:T(8,128)S(1)} %get-tuple-element.21, f32[32,4096]{1,0:T(8,128)S(1)} %get-tuple-element.20, f32[32,4096]{1,0:T(8,128)S(1)} %get-tuple-element.19, f32[32,4096]{1,0:T(8,128)S(1)} %get-tuple-element.18, ...), kind=kLoop, calls=%fused_computation.156 | loop fusion | flops 5636096 | bytes 10813524 | tf_op jit(solution)/shard_map/add | solution.py:34
  68.5 14.1 %multiply_add_fusion.2 = f32[32,4096]{1,0:T(8,128)S(1)} fusion(f32[32,4096]{1,0:T(8,128)S(1)} %get-tuple-element.22, f32[32,4096]{1,0:T(8,128)S(1)} %get-tuple-element.21, f32[32,4096]{1,0:T(8,128)S(1)} %get-tuple-element.20, f32[32,4096]{1,0:T(8,128)S(1)} %get-tuple-element.19, f32[32,4096]{1,0:T(8,128)S(1)} %get-tuple-element.18, ...), kind=kLoop, calls=%fused_computation.129 | loop fusion | flops 5636096 | bytes 10813524 | tf_op jit(solution)/shard_map/add | solution.py:34
  82.5 14.9 %multiply_add_fusion.1 = f32[32,4096]{1,0:T(8,128)} fusion(f32[32,4096]{1,0:T(8,128)S(1)} %get-tuple-element.22, f32[32,4096]{1,0:T(8,128)S(1)} %get-tuple-element.21, f32[32,4096]{1,0:T(8,128)S(1)} %get-tuple-element.20, f32[32,4096]{1,0:T(8,128)S(1)} %get-tuple-element.19, f32[32,4096]{1,0:T(8,128)S(1)} %get-tuple-element.18, ...), kind=kLoop, calls=%fused_computation.102 | loop fusion | flops 5636096 | bytes 10813524 | tf_op jit(solution)/shard_map/add | solution.py:34
  97.4 89.2 %multiply_add_fusion = f32[32,4096]{1,0:T(8,128)S(1)} fusion(f32[32,4096]{1,0:T(8,128)} %multiply_add_fusion.1, f32[32,4096]{1,0:T(8,128)S(1)} %multiply_add_fusion.2, f32[32,4096]{1,0:T(8,128)S(1)} %multiply_add_fusion.3, f32[32,4096]{1,0:T(8,128)S(1)} %multiply_add_fusion.4, f32[32,4096]{1,0:T(8,128)S(1)} %get-tuple-element.4, f32[]{:T(128)} %bitcast.225, ...), kind=kLoop, calls=%fused_computation.75 | loop fusion | flops 28049408 | bytes 3146168 | tf_op jit(solution)/shard_map/add | solution.py:39
  186.5 1.4 fusion.115
  188.0 4.2 %collective-permute-start.2 = (bf16[2,32,4096]{2,1,0:T(8,128)(2,1)S(1)}, bf16[2,32,4096]{2,1,0:T(8,128)(2,1)S(1)}, u32[]{:S(2)}, u32[]{:S(2)}) collective-permute-start(bf16[2,32,4096]{2,1,0:T(8,128)(2,1)S(1)} %pad_maximum_fusion.2), channel_id=1, source_target_pairs={{0,1},{1,2},{2,3},{3,4},{4,5},{5,6},{6,7},{7,8},{8,9},{9,10},{10,1... | collective-permute-start | bytes 1572872 | tf_op jit(solution)/shard_map/ppermute | solution.py:23
  192.9 9.4 %collective-permute-done.2 = bf16[2,32,4096]{2,1,0:T(8,128)(2,1)S(1)} collective-permute-done((bf16[2,32,4096]{2,1,0:T(8,128)(2,1)S(1)}, bf16[2,32,4096]{2,1,0:T(8,128)(2,1)S(1)}, u32[]{:S(2)}, u32[]{:S(2)}) %collective-permute-start.2) | collective-permute-done | bytes 524320 | tf_op jit(solution)/shard_map/ppermute | solution.py:23
  202.4 6.3 %collective-permute-start.3 = (bf16[2,32,4096]{2,1,0:T(8,128)(2,1)S(1)}, bf16[2,32,4096]{2,1,0:T(8,128)(2,1)S(1)}, u32[]{:S(2)}, u32[]{:S(2)}) collective-permute-start(bf16[2,32,4096]{2,1,0:T(8,128)(2,1)S(1)} %broadcast_select_fusion), channel_id=1, source_target_pairs={{0,2},{1,3},{2,4},{3,5},{4,6},{5,7},{6,8},{7,9},{8,10},{9,11},{10,... | collective-permute-start | bytes 1572872 | tf_op jit(solution)/shard_map/ppermute | solution.py:23
  208.7 20.6 %collective-permute-done.3 = bf16[2,32,4096]{2,1,0:T(8,128)(2,1)S(1)} collective-permute-done((bf16[2,32,4096]{2,1,0:T(8,128)(2,1)S(1)}, bf16[2,32,4096]{2,1,0:T(8,128)(2,1)S(1)}, u32[]{:S(2)}, u32[]{:S(2)}) %collective-permute-start.3) | collective-permute-done | bytes 524320 | tf_op jit(solution)/shard_map/ppermute | solution.py:23
  229.3 13.2 %collective-permute-start.4 = (bf16[2,32,4096]{2,1,0:T(8,128)(2,1)S(1)}, bf16[2,32,4096]{2,1,0:T(8,128)(2,1)S(1)}, u32[]{:S(2)}, u32[]{:S(2)}) collective-permute-start(bf16[2,32,4096]{2,1,0:T(8,128)(2,1)S(1)} %broadcast_select_fusion.1), channel_id=1, source_target_pairs={{0,4},{1,5},{2,6},{3,7},{4,8},{5,9},{6,10},{7,11},{8,12},{9,13},{1... | collective-permute-start | bytes 1572872 | tf_op jit(solution)/shard_map/ppermute | solution.py:23
  242.5 22.1 %collective-permute-done.4 = bf16[2,32,4096]{2,1,0:T(8,128)(2,1)S(1)} collective-permute-done((bf16[2,32,4096]{2,1,0:T(8,128)(2,1)S(1)}, bf16[2,32,4096]{2,1,0:T(8,128)(2,1)S(1)}, u32[]{:S(2)}, u32[]{:S(2)}) %collective-permute-start.4) | collective-permute-done | bytes 524320 | tf_op jit(solution)/shard_map/ppermute | solution.py:23
  264.6 5.8 %collective-permute-start.5 = (bf16[2,32,4096]{2,1,0:T(8,128)(2,1)S(1)}, bf16[2,32,4096]{2,1,0:T(8,128)(2,1)S(1)}, u32[]{:S(2)}, u32[]{:S(2)}) collective-permute-start(bf16[2,32,4096]{2,1,0:T(8,128)(2,1)S(1)} %broadcast_select_fusion.2), channel_id=1, source_target_pairs={{0,8},{1,9},{2,10},{3,11},{4,12},{5,13},{6,14},{7,15},{8,16},{9,17... | collective-permute-start | bytes 1572872 | tf_op jit(solution)/shard_map/ppermute | solution.py:23
  270.4 10.7 %collective-permute-done.5 = bf16[2,32,4096]{2,1,0:T(8,128)(2,1)S(1)} collective-permute-done((bf16[2,32,4096]{2,1,0:T(8,128)(2,1)S(1)}, bf16[2,32,4096]{2,1,0:T(8,128)(2,1)S(1)}, u32[]{:S(2)}, u32[]{:S(2)}) %collective-permute-start.5) | collective-permute-done | bytes 524320 | tf_op jit(solution)/shard_map/ppermute | solution.py:23
  281.2 5.7 %collective-permute-start.6 = (bf16[2,32,4096]{2,1,0:T(8,128)(2,1)S(1)}, bf16[2,32,4096]{2,1,0:T(8,128)(2,1)S(1)}, u32[]{:S(2)}, u32[]{:S(2)}) collective-permute-start(bf16[2,32,4096]{2,1,0:T(8,128)(2,1)S(1)} %broadcast_select_fusion.3), channel_id=1, source_target_pairs={{0,16},{1,17},{2,18},{3,19},{4,20},{5,21},{6,22},{7,23},{8,24},{9,... | collective-permute-start | bytes 1572872 | tf_op jit(solution)/shard_map/ppermute | solution.py:23
  286.9 9.8 %collective-permute-done.6 = bf16[2,32,4096]{2,1,0:T(8,128)(2,1)S(1)} collective-permute-done((bf16[2,32,4096]{2,1,0:T(8,128)(2,1)S(1)}, bf16[2,32,4096]{2,1,0:T(8,128)(2,1)S(1)}, u32[]{:S(2)}, u32[]{:S(2)}) %collective-permute-start.6) | collective-permute-done | bytes 524320 | tf_op jit(solution)/shard_map/ppermute | solution.py:23
  296.8 1.3 collective-permute-start.7
  298.8 8.5 %collective-permute-done.7 = bf16[2,32,4096]{2,1,0:T(8,128)(2,1)S(1)} collective-permute-done((bf16[2,32,4096]{2,1,0:T(8,128)(2,1)S(1)}, bf16[2,32,4096]{2,1,0:T(8,128)(2,1)S(1)}, u32[]{:S(2)}, u32[]{:S(2)}) %collective-permute-start.7) | collective-permute-done | bytes 524320 | tf_op jit(solution)/shard_map/ppermute | solution.py:23
  307.7 4.1 %collective-permute-start.8 = (bf16[3,4096]{1,0:T(4,128)(2,1)S(1)}, bf16[3,4096]{1,0:T(4,128)(2,1)S(1)}, u32[]{:S(2)}, u32[]{:S(2)}) collective-permute-start(bf16[3,4096]{1,0:T(4,128)(2,1)S(1)} %get-tuple-element.26), channel_id=1, source_target_pairs={{0,1},{1,2},{2,3},{3,4},{4,5},{5,6},{6,7},{7,8},{8,9},{9,10},{10,1... | collective-permute-start | bytes 73736 | tf_op jit(solution)/shard_map/ppermute | solution.py:14
  311.8 1.3 collective-permute-start.9
  313.1 0.8 fusion.114
  314.0 2.5 collective-permute-done.9
  316.5 1.3 add_multiply_fusion
  317.8 74.9 %all-reduce.9.cloned.1.call-done = (f32[32,4096]{1,0:T(8,128)}, f32[32,4096]{1,0:T(8,128)}) async-done(((f32[32,4096]{1,0:T(8,128)}, f32[32,4096]{1,0:T(8,128)}), (f32[32,4096]{1,0:T(8,128)}, f32[32,4096]{1,0:T(8,128)})) %all-reduce.9.cloned.1.call-update) | async-done | bytes 1048592 | tf_op jit(solution)/shard_map/psum | solution.py:100
  392.7 2.1 maximum_divide_fusion
  394.8 0.8 copy.15
  (51 shorter events, 11.1 us)
Async XLA Ops:
  7.2 385.5 %all-reduce.9.cloned.1.call-start = ((), (), s32[]{:S(2)}) async-start(), calls=%async_computation | async-start | bytes 2097152 | tf_op jit(solution)/shard_map/psum | solution.py:100
  7.2 7.0 %copy-start.4 = (f32[5,21]{1,0:T(8,128)S(1)}, f32[5,21]{1,0:T(8,128)}, u32[]{:S(2)}) copy-start(f32[5,21]{1,0:T(8,128)} %param.15) | copy-start | bytes 1264
  7.2 10.6 %copy-start.3 = (f32[5,21]{1,0:T(8,128)S(1)}, f32[5,21]{1,0:T(8,128)}, u32[]{:S(2)}) copy-start(f32[5,21]{1,0:T(8,128)} %param.16) | copy-start | bytes 1264
  7.2 14.9 %copy-start.6 = (s32[1,4096]{1,0:T(1,128)S(1)}, s32[1,4096]{1,0:T(1,128)}, u32[]{:S(2)}) copy-start(s32[1,4096]{1,0:T(1,128)} %param.18) | copy-start | bytes 49156
  8.3 13.8 %copy-start.2 = (f32[1,6,4096]{2,0,1:T(1,128)S(1)}, f32[1,6,4096]{2,0,1:T(1,128)}, u32[]{:S(2)}) copy-start(f32[1,6,4096]{2,0,1:T(1,128)} %param.17) | copy-start | bytes 294916
  8.3 15.0 %copy-start.5 = (f32[1,32,4096]{2,1,0:T(8,128)S(1)}, f32[1,32,4096]{2,1,0:T(8,128)}, u32[]{:S(2)}) copy-start(f32[1,32,4096]{2,1,0:T(8,128)} %param.11) | copy-start | bytes 1572868
  8.3 17.0 %collective-permute-start = (f32[10,4096]{1,0:T(8,128)S(1)}, f32[10,4096]{1,0:T(8,128)S(1)}, u32[]{:S(2)}, u32[]{:S(2)}) collective-permute-start(f32[10,4096]{1,0:T(8,128)S(1)} %get-tuple-element.28), channel_id=1, source_target_pairs={{0,1},{1,2},{2,3},{3,4},{4,5},{5,6},{6,7},{7,8},{8,9},{9,10},{10,1... | collective-permute-start | bytes 491528 | tf_op jit(solution)/shard_map/ppermute | solution.py:14
  12.9 12.5 %collective-permute-start.1 = (f32[10,4096]{1,0:T(8,128)S(1)}, f32[10,4096]{1,0:T(8,128)S(1)}, u32[]{:S(2)}, u32[]{:S(2)}) collective-permute-start(f32[10,4096]{1,0:T(8,128)S(1)} %get-tuple-element.27), channel_id=1, source_target_pairs={{1,0},{2,1},{3,2},{4,3},{5,4},{6,5},{7,6},{8,7},{9,8},{10,9},{11,1... | collective-permute-start | bytes 491528 | tf_op jit(solution)/shard_map/ppermute | solution.py:15
  22.7 0.7 copy-start.9
  23.0 2.4 copy-start
  23.4 0.7 copy-start.7
  188.0 14.3 %collective-permute-start.2 = (bf16[2,32,4096]{2,1,0:T(8,128)(2,1)S(1)}, bf16[2,32,4096]{2,1,0:T(8,128)(2,1)S(1)}, u32[]{:S(2)}, u32[]{:S(2)}) collective-permute-start(bf16[2,32,4096]{2,1,0:T(8,128)(2,1)S(1)} %pad_maximum_fusion.2), channel_id=1, source_target_pairs={{0,1},{1,2},{2,3},{3,4},{4,5},{5,6},{6,7},{7,8},{8,9},{9,10},{10,1... | collective-permute-start | bytes 1572872 | tf_op jit(solution)/shard_map/ppermute | solution.py:23
  202.4 26.8 %collective-permute-start.3 = (bf16[2,32,4096]{2,1,0:T(8,128)(2,1)S(1)}, bf16[2,32,4096]{2,1,0:T(8,128)(2,1)S(1)}, u32[]{:S(2)}, u32[]{:S(2)}) collective-permute-start(bf16[2,32,4096]{2,1,0:T(8,128)(2,1)S(1)} %broadcast_select_fusion), channel_id=1, source_target_pairs={{0,2},{1,3},{2,4},{3,5},{4,6},{5,7},{6,8},{7,9},{8,10},{9,11},{10,... | collective-permute-start | bytes 1572872 | tf_op jit(solution)/shard_map/ppermute | solution.py:23
  229.3 35.2 %collective-permute-start.4 = (bf16[2,32,4096]{2,1,0:T(8,128)(2,1)S(1)}, bf16[2,32,4096]{2,1,0:T(8,128)(2,1)S(1)}, u32[]{:S(2)}, u32[]{:S(2)}) collective-permute-start(bf16[2,32,4096]{2,1,0:T(8,128)(2,1)S(1)} %broadcast_select_fusion.1), channel_id=1, source_target_pairs={{0,4},{1,5},{2,6},{3,7},{4,8},{5,9},{6,10},{7,11},{8,12},{9,13},{1... | collective-permute-start | bytes 1572872 | tf_op jit(solution)/shard_map/ppermute | solution.py:23
  264.6 16.6 %collective-permute-start.5 = (bf16[2,32,4096]{2,1,0:T(8,128)(2,1)S(1)}, bf16[2,32,4096]{2,1,0:T(8,128)(2,1)S(1)}, u32[]{:S(2)}, u32[]{:S(2)}) collective-permute-start(bf16[2,32,4096]{2,1,0:T(8,128)(2,1)S(1)} %broadcast_select_fusion.2), channel_id=1, source_target_pairs={{0,8},{1,9},{2,10},{3,11},{4,12},{5,13},{6,14},{7,15},{8,16},{9,17... | collective-permute-start | bytes 1572872 | tf_op jit(solution)/shard_map/ppermute | solution.py:23
  281.2 15.5 %collective-permute-start.6 = (bf16[2,32,4096]{2,1,0:T(8,128)(2,1)S(1)}, bf16[2,32,4096]{2,1,0:T(8,128)(2,1)S(1)}, u32[]{:S(2)}, u32[]{:S(2)}) collective-permute-start(bf16[2,32,4096]{2,1,0:T(8,128)(2,1)S(1)} %broadcast_select_fusion.3), channel_id=1, source_target_pairs={{0,16},{1,17},{2,18},{3,19},{4,20},{5,21},{6,22},{7,23},{8,24},{9,... | collective-permute-start | bytes 1572872 | tf_op jit(solution)/shard_map/ppermute | solution.py:23
  296.8 10.5 %collective-permute-start.7 = (bf16[2,32,4096]{2,1,0:T(8,128)(2,1)S(1)}, bf16[2,32,4096]{2,1,0:T(8,128)(2,1)S(1)}, u32[]{:S(2)}, u32[]{:S(2)}) collective-permute-start(bf16[2,32,4096]{2,1,0:T(8,128)(2,1)S(1)} %broadcast_select_fusion.4), channel_id=1, source_target_pairs={{0,1},{1,2},{2,3},{3,4},{4,5},{5,6},{6,7},{7,8},{8,9},{9,10},{10,1... | collective-permute-start | bytes 1572872 | tf_op jit(solution)/shard_map/ppermute | solution.py:23
  298.1 0.7 copy-start.8
  307.7 6.3 %collective-permute-start.8 = (bf16[3,4096]{1,0:T(4,128)(2,1)S(1)}, bf16[3,4096]{1,0:T(4,128)(2,1)S(1)}, u32[]{:S(2)}, u32[]{:S(2)}) collective-permute-start(bf16[3,4096]{1,0:T(4,128)(2,1)S(1)} %get-tuple-element.26), channel_id=1, source_target_pairs={{0,1},{1,2},{2,3},{3,4},{4,5},{5,6},{6,7},{7,8},{8,9},{9,10},{10,1... | collective-permute-start | bytes 73736 | tf_op jit(solution)/shard_map/ppermute | solution.py:14
  311.8 4.7 %collective-permute-start.9 = (bf16[3,4096]{1,0:T(4,128)(2,1)S(1)}, bf16[3,4096]{1,0:T(4,128)(2,1)S(1)}, u32[]{:S(2)}, u32[]{:S(2)}) collective-permute-start(bf16[3,4096]{1,0:T(4,128)(2,1)S(1)} %get-tuple-element.25), channel_id=1, source_target_pairs={{1,0},{2,1},{3,2},{4,3},{5,4},{6,5},{7,6},{8,7},{9,8},{10,9},{11,1... | collective-permute-start | bytes 73736 | tf_op jit(solution)/shard_map/ppermute | solution.py:15
  392.7 2.1 copy-start.1
Sparse Core Ops, SparseCore 0:
  317.9 74.6 all-reduce.8
where the time goes:
time: 406 us; the launch traced here: 402 us
  other arithmetic  169 us (42%)
  waiting for transfers between devices  159 us (39%)
  starting transfers between devices  47.7 us (12%)
  between operations  15 us (4%)
  local copies, waits for them, and re-layouts  12.7 us (3%)
    add x1, other arithmetic, match_psf(): result = result + weights[basis] * col_pass  89.2 us
    ppermute x6, waiting for transfers between devices, passed_along(): return lax.ppermute(x, axis, pairs)  81.1 us
    psum x1, waiting for transfers between devices, body(): total_numer, total_denom = lax.psum((numer, sky_ivar), 'visit')  74.9 us
    add x5, other arithmetic, match_psf(): row_pass = row_pass + vertical[basis, offset] * padded[offset:offset + rows]  71.9 us
    ppermute x6, starting transfers between devices, passed_along(): return lax.ppermute(x, axis, pairs)  36.4 us
    ppermute x2, starting transfers between devices, with_halo(): before = lax.ppermute(last, axis, up)  8.62 us
  transfers between devices with their start and end apart: 11, of which 8 were waited for; matrix products, arithmetic and copies ran while one was open for 3% of the time, Pallas kernels for 0%

commit v1 on v0

v1 whole, which is shorter than its diff:
```python
import functools

import jax
import jax.numpy as jnp
from jax import lax
from jax.experimental import pallas as pl
from jax.experimental.pallas import tpu as pltpu
from jax.sharding import PartitionSpec as P

MESH = pl.DeviceIdType.MESH
F32 = jnp.float32
BF16 = jnp.bfloat16
TAPS = 21
RIM = 10
BASES = 5
LANCZOS = 6
BLOCK = 32
SLAB = 128
PAD = 520


def split(x):
    high = x.astype(BF16)
    return high, (x - high.astype(F32)).astype(BF16)


def kernel(
    nv, nt,
    image, variance, mask, shift, coef, vert, horiz, colw, coloff, roww,
    out_c, out_w,
    x_cat, v_mat, e_hi, e_lo, o_hi, o_lo, t_main_hi, t_main_lo, t_halo_hi, t_halo_lo,
    matched, factor, rw_pad, s_iv, r_iv, s_cw, r_cw, ivf, cwf, wbi,
    nb_iv, nb_nu, c2_iv, c2_nu, total_iv, c3_iv, c3_nu, f_iv, f_nu,
    halo_send, halo_recv, send_sem, recv_sem,
):
    v, t = lax.axis_index("visit"), lax.axis_index("tile")
    depth = nt // 8
    per = nt // nv
    groups = nt // 4
    pairs = nt // 2
    rows_all = nt * BLOCK
    half = lax.rem(v, 2)
    quarter = lax.div(v, 2)
    owner = lax.div(t, per)
    to_self = (owner == v) & (lax.rem(t, 4) == quarter)

    barrier = pltpu.get_barrier_semaphore()

    def greet(v2, t2):
        pl.semaphore_signal(barrier, inc=1, device_id=(v2, t2), device_id_type=MESH)

    def greet_tile(k, c):
        greet(v, lax.rem(t + k, nt))
        return c

    def greet_visit(k, c):
        greet(lax.rem(v + k, nv), t)
        return c

    def greet_source(k, c):
        v2 = 2 * lax.rem(t, 4) + lax.rem(k, 2)
        t2 = per * v + lax.div(k, 2)

        @pl.when(jnp.logical_not((v2 == v) & (t2 == t)))
        def _():
            greet(v2, t2)

        return c

    lax.fori_loop(1, nt, greet_tile, 0)
    lax.fori_loop(1, nv, greet_visit, 0)
    lax.fori_loop(0, 2 * per, greet_source, 0)

    def cols(j, n=SLAB):
        return pl.ds(pl.multiple_of(j * n, n), n)

    def fill(j, c):
        high, low = split(image[0, :, cols(j)])
        x_cat[16:48, cols(j)] = high
        x_cat[64:96, cols(j)] = low
        x_cat[112:144, cols(j)] = high
        return c

    lax.fori_loop(0, nt, fill, 0)
    pl.semaphore_wait(barrier, (nt - 1) + (nv - 1) + groups - to_self.astype(jnp.int32))

    up = pltpu.make_async_remote_copy(
        src_ref=x_cat.at[pl.ds(32, 16)], dst_ref=x_cat.at[pl.ds(0, 16)],
        send_sem=halo_send.at[0], recv_sem=halo_recv.at[0],
        device_id=(v, lax.rem(t + 1, nt)), device_id_type=MESH)
    down = pltpu.make_async_remote_copy(
        src_ref=x_cat.at[pl.ds(16, 16)], dst_ref=x_cat.at[pl.ds(48, 16)],
        send_sem=halo_send.at[1], recv_sem=halo_recv.at[1],
        device_id=(v, lax.rem(t + nt - 1, nt)), device_id_type=MESH)
    up.start()
    down.start()

    flags = jnp.broadcast_to(mask[...].astype(F32), (BLOCK, BLOCK))
    same = lax.broadcasted_iota(jnp.int32, (BLOCK, BLOCK), 0) == lax.broadcasted_iota(jnp.int32, (BLOCK, BLOCK), 1)
    usable = jnp.sum(jnp.where(same, flags, 0.0), axis=1, keepdims=True)
    rw_pad[...] = jnp.zeros_like(rw_pad)
    for q in range(4):
        rw_pad[0:LANCZOS, BLOCK * q:BLOCK * (q + 1)] = roww[0]
    lane = lax.broadcasted_iota(jnp.int32, (8, SLAB), 1)
    placed = jnp.where(lax.div(lane, BLOCK) == lax.rem(t, 4), rw_pad[...], 0.0)
    placed_hi = placed.astype(BF16).astype(F32)
    packed = jnp.concatenate([placed_hi, placed - placed_hi], axis=0).astype(BF16)

    def weigh(j, c):
        s_iv[j, 0:BLOCK, :] = (usable / variance[0, :, cols(j)]).astype(BF16)
        s_iv[j, BLOCK:48, :] = packed
        return c

    lax.fori_loop(0, nt, weigh, 0)

    def exchange(source, target, at):
        def step(k, c):
            x = lax.rem(lax.div(t, 8) + lax.div(k, 8), depth)
            z = lax.rem(lax.rem(t, 8) + 3 * k, 8)
            t2 = x * 8 + z
            pltpu.make_async_remote_copy(
                src_ref=source.at[t2], dst_ref=target.at[t],
                send_sem=send_sem.at[at], recv_sem=recv_sem.at[at],
                device_id=(v, t2), device_id_type=MESH).start()
            return c

        lax.fori_loop(1, nt, step, 0)
        target[t] = source[t]

    def arrived(ref, at):
        pltpu.make_async_copy(ref, ref, recv_sem.at[at]).wait()

    def left(ref, at):
        pltpu.make_async_copy(ref, ref, send_sem.at[at]).wait()

    exchange(s_iv, r_iv, 0)

    r_at = lax.broadcasted_iota(jnp.int32, (BLOCK, 160), 0)
    q_at = lax.broadcasted_iota(jnp.int32, (BLOCK, 160), 1)
    q_row = jnp.where(q_at < 64, q_at - 16, jnp.where(q_at < 96, q_at - 64, q_at - 112))
    tap = q_row - r_at + RIM
    for b in range(BASES):
        value = jnp.zeros((BLOCK, 160), F32)
        for i in range(TAPS):
            value = jnp.where(tap == i, coef[0, b] * vert[b, i], value)
        high = value.astype(BF16).astype(F32)
        v_mat[BLOCK * b:BLOCK * (b + 1), :] = jnp.where(q_at < 96, high, value - high).astype(BF16)

    n_at = lax.broadcasted_iota(jnp.int32, (16, 256), 1)
    k_at = lax.broadcasted_iota(jnp.int32, (16, 256), 0)

    def band(d):
        values = [jnp.zeros((16, 256), F32) for _ in range(BASES)]
        for i in range(TAPS):
            hit = d == i
            values = [jnp.where(hit, horiz[b, i], values[b]) for b in range(BASES)]
        return [split(value) for value in values]

    def build(c, carry):
        parts = band(16 * c + k_at - n_at + RIM)
        at = pl.ds(pl.multiple_of(16 * c, 16), 16)
        for b in range(BASES):
            t_main_hi[b, at, :], t_main_lo[b, at, :] = parts[b]
            t_halo_hi[b, at, :] = jnp.zeros((16, 256), BF16)
            t_halo_lo[b, at, :] = jnp.zeros((16, 256), BF16)
        return carry

    lax.fori_loop(0, 16, build, 0)
    for start, gap in ((112, -118), (128, 138)):
        parts = band(start + k_at - n_at + gap)
        for b in range(BASES):
            t_halo_hi[b, start:start + 16, :], t_halo_lo[b, start:start + 16, :] = parts[b]

    c_at = lax.broadcasted_iota(jnp.int32, (1, 512), 1)

    def weights(g, c):
        delta = coloff[0:1, cols(g, 512)] - (c_at + 512 * g)
        sums = [jnp.zeros((1, 512), F32) for _ in range(11)]
        for gap in range(-5, 1):
            hit = delta == gap
            for k in range(LANCZOS):
                sums[gap + k + 5] = sums[gap + k + 5] + jnp.where(hit, colw[0, k:k + 1, cols(g, 512)], 0.0)
        for d in range(11):
            factor[d:d + 1, cols(g, 512)] = sums[d]
        return c

    lax.fori_loop(0, groups, weights, 0)

    for ref in (e_hi, e_lo):
        ref[:, pairs] = jnp.zeros((BASES, BLOCK, SLAB), BF16)
    for ref in (o_hi, o_lo):
        ref[:, 0] = jnp.zeros((BASES, BLOCK, SLAB), BF16)
    matched[:, 0:SLAB] = jnp.zeros((BLOCK, SLAB), F32)
    matched[:, SLAB + nt * SLAB:] = jnp.zeros((BLOCK, SLAB), F32)
    for ref in (ivf, cwf):
        ref[0:PAD, :] = jnp.zeros((PAD, SLAB), F32)
        ref[PAD + rows_all:, :] = jnp.zeros((8, SLAB), F32)

    up.wait_recv()
    down.wait_recv()

    @pl.when(t == 0)
    def _():
        x_cat[0:16, :] = jnp.zeros((16, nt * SLAB), BF16)

    @pl.when(t == nt - 1)
    def _():
        x_cat[48:64, :] = jnp.zeros((16, nt * SLAB), BF16)

    x_cat[96:112, :] = x_cat[0:16, :]
    x_cat[144:160, :] = x_cat[48:64, :]

    def vertical(j, c):
        passed = jnp.dot(v_mat[...], x_cat[:, cols(j, 256)], preferred_element_type=F32)
        for b in range(BASES):
            high, low = split(passed[BLOCK * b:BLOCK * (b + 1)])
            e_hi[b, j], o_hi[b, j + 1] = high[:, :SLAB], high[:, SLAB:]
            e_lo[b, j], o_lo[b, j + 1] = low[:, :SLAB], low[:, SLAB:]
        return c

    lax.fori_loop(0, pairs, vertical, 0)

    def horizontal(g, c):
        def side(ref, b, start):
            return ref[b, pl.ds(4 * g + start, 4)].reshape(4 * BLOCK, SLAB)

        total = jnp.zeros((4 * BLOCK, 256), F32)
        for b in range(BASES):
            main_hi = jnp.concatenate([side(e_hi, b, 0), side(o_hi, b, 1)], axis=1)
            main_lo = jnp.concatenate([side(e_lo, b, 0), side(o_lo, b, 1)], axis=1)
            halo_hi = jnp.concatenate([side(o_hi, b, 0), side(e_hi, b, 1)], axis=1)
            halo_lo = jnp.concatenate([side(o_lo, b, 0), side(e_lo, b, 1)], axis=1)
            for left_side, right_side in (
                (main_hi, t_main_hi), (main_lo, t_main_hi), (main_hi, t_main_lo),
                (halo_hi, t_halo_hi), (halo_lo, t_halo_hi), (halo_hi, t_halo_lo),
            ):
                total = total + jnp.dot(left_side, right_side[b], preferred_element_type=F32)
        for i in range(4):
            at = pl.ds(pl.multiple_of(1024 * g + 256 * i + SLAB, SLAB), 256)
            matched[:, at] = total[BLOCK * i:BLOCK * (i + 1)]
        return c

    lax.fori_loop(0, pairs // 4, horizontal, 0)

    def interpolate(g, c):
        for r in range(2):
            window = matched[16 * r:16 * (r + 1), pl.ds(pl.multiple_of(512 * g, 512), 768)]
            total = jnp.zeros((16, 512), F32)
            for d in range(-5, 6):
                moved = pltpu.roll(window, (-d) % 768, 1) if d else window
                total = total + factor[d + 5:d + 6, cols(g, 512)] * moved[:, SLAB:SLAB + 512]
            total = total.astype(BF16)
            for i in range(4):
                s_cw[4 * g + i, 16 * r:16 * (r + 1), :] = total[:, SLAB * i:SLAB * (i + 1)]
        return c

    lax.fori_loop(0, groups, interpolate, 0)
    exchange(s_cw, r_cw, 1)

    arrived(r_iv.at[pl.ds(0, nt - 1)], 0)

    def unpack(ref, target):
        def step(j, c):
            target[pl.ds(pl.multiple_of(PAD + BLOCK * j, 8), BLOCK), :] = ref[j, 0:BLOCK, :].astype(F32)
            return c

        lax.fori_loop(0, nt, step, 0)

    unpack(r_iv, ivf)
    amount = shift[0]
    pick = lax.broadcasted_iota(jnp.int32, (16, LANCZOS * SLAB), 0)
    pick = lax.rem(pick, 8) == lax.div(lax.broadcasted_iota(jnp.int32, (16, LANCZOS * SLAB), 1), SLAB)
    pick = pick.astype(F32).astype(BF16)
    row_at = lax.broadcasted_iota(jnp.int32, (SLAB, SLAB), 0)

    def spread(g, c):
        pieces = [r_iv[4 * g + q, BLOCK:48, :].astype(F32) for q in range(4)]
        joined = (pieces[0] + pieces[1] + pieces[2] + pieces[3]).astype(BF16)
        wide = lax.dot_general(joined, pick, (((0,), (0,)), ((), ())), preferred_element_type=F32)
        sky = ivf[pl.ds(SLAB * g + PAD - amount, SLAB), :]
        nb_iv[g] = sky.astype(BF16).reshape(8, 16, SLAB)
        for k in range(LANCZOS):
            inside = row_at + (SLAB * g + k - 2) < rows_all
            wbi[k, cols(g), :] = jnp.where(inside, wide[:, SLAB * k:SLAB * (k + 1)] * sky, 0.0)
        return c

    lax.fori_loop(0, groups, spread, 0)

    def scatter(source, target, at):
        def step(k, c):
            v2 = lax.rem(v + k, nv)
            pltpu.make_async_remote_copy(
                src_ref=source.at[:, v2], dst_ref=target.at[v],
                send_sem=send_sem.at[at], recv_sem=recv_sem.at[at],
                device_id=(v2, t), device_id_type=MESH).start()
            return c

        lax.fori_loop(1, nv, step, 0)
        target[v] = source[:, v]

    def deliver(source, target, at):
        rows = pl.ds(pl.multiple_of(16 * half, 16), 16)

        def step(i, c):
            t2 = 4 * i + quarter
            me = (owner == v) & (t2 == t)

            @pl.when(jnp.logical_not(me))
            def _():
                pltpu.make_async_remote_copy(
                    src_ref=source.at[i], dst_ref=target.at[t, rows],
                    send_sem=send_sem.at[at], recv_sem=recv_sem.at[at],
                    device_id=(owner, t2), device_id_type=MESH).start()

            @pl.when(me)
            def _():
                pltpu.make_async_copy(source.at[i], target.at[t, rows], recv_sem.at[at]).start()

            return c

        lax.fori_loop(0, groups, step, 0)

    def gather(target, at):
        mine = target.at[pl.ds(per * v, per)]

        def step(k, c):
            pltpu.make_async_remote_copy(
                src_ref=mine, dst_ref=mine,
                send_sem=send_sem.at[at], recv_sem=recv_sem.at[at],
                device_id=(lax.rem(v + k, nv), t), device_id_type=MESH).start()
            return c

        lax.fori_loop(1, nv, step, 0)

    def summed(ref, i):
        total = ref[0, i].astype(F32)
        for u in range(1, nv):
            total = total + ref[u, i].astype(F32)
        return total

    scatter(nb_iv, c2_iv, 2)
    arrived(c2_iv.at[pl.ds(0, nv - 1)], 2)

    def add_iv(i, c):
        total = summed(c2_iv, i)
        total_iv[i] = total
        c3_iv[i] = total.astype(BF16)
        return c

    lax.fori_loop(0, groups, add_iv, 0)
    deliver(c3_iv, f_iv, 3)
    arrived(f_iv.at[pl.ds(0, per)], 3)
    gather(f_iv, 4)

    arrived(r_cw.at[pl.ds(0, nt - 1)], 1)
    unpack(r_cw, cwf)

    def warp(g, c):
        total = jnp.zeros((SLAB, SLAB), F32)
        for k in range(LANCZOS):
            total = total + wbi[k, cols(g), :] * cwf[pl.ds(SLAB * g + PAD + k - 2 - amount, SLAB), :]
        nb_nu[g] = total.astype(BF16).reshape(8, 16, SLAB)
        return c

    lax.fori_loop(0, groups, warp, 0)
    scatter(nb_nu, c2_nu, 5)
    arrived(c2_nu.at[pl.ds(0, nv - 1)], 5)

    def add_nu(i, c):
        c3_nu[i] = (summed(c2_nu, i) / jnp.maximum(total_iv[i], 1.0)).astype(BF16)
        return c

    lax.fori_loop(0, groups, add_nu, 0)
    deliver(c3_nu, f_nu, 6)
    arrived(f_nu.at[pl.ds(0, per)], 6)
    gather(f_nu, 7)

    def emit(ref, out):
        def step(j, c):
            out[:, cols(j)] = ref[j].astype(F32)
            return c

        lax.fori_loop(0, nt, step, 0)

    arrived(f_iv.at[pl.ds(0, (nv - 1) * per)], 4)
    emit(f_iv, out_w)
    arrived(f_nu.at[pl.ds(0, (nv - 1) * per)], 7)
    emit(f_nu, out_c)

    up.wait_send()
    down.wait_send()
    left(s_iv.at[pl.ds(0, nt - 1)], 0)
    left(s_cw.at[pl.ds(0, nt - 1)], 1)
    for source, c3, final, at in ((c2_iv, c3_iv, f_iv, 2), (c2_nu, c3_nu, f_nu, 5)):
        left(source.at[pl.ds(0, nv - 1)], at)

        @pl.when(to_self)
        def _():
            left(c3.at[pl.ds(0, groups - 1)], at + 1)

        @pl.when(jnp.logical_not(to_self))
        def _():
            left(c3, at + 1)

        left(final.at[pl.ds(0, (nv - 1) * per)], at + 2)


def solution(mesh):
    nv, nt = mesh.shape["visit"], mesh.shape["tile"]
    width = nt * SLAB
    groups, pairs, per = nt // 4, nt // 2, nt // nv

    def body(*args):
        vmem = pl.BlockSpec(memory_space=pltpu.VMEM)
        smem = pl.BlockSpec(memory_space=pltpu.SMEM)

        def plane(*shape, dtype=BF16):
            return pltpu.VMEM(shape, dtype)

        return pl.pallas_call(
            functools.partial(kernel, nv, nt),
            out_shape=[jax.ShapeDtypeStruct((BLOCK, width), F32)] * 2,
            in_specs=[vmem, vmem, vmem, smem, smem, smem, smem, vmem, vmem, vmem],
            out_specs=[vmem, vmem],
            scratch_shapes=[
                plane(160, width),
                plane(160, 160),
                *[plane(BASES, pairs + 1, BLOCK, SLAB)] * 4,
                *[plane(BASES, 256, 256)] * 4,
                plane(BLOCK, width + 2 * SLAB, dtype=F32),
                plane(16, width, dtype=F32),
                plane(8, SLAB, dtype=F32),
                plane(nt, 48, SLAB), plane(nt, 48, SLAB),
                plane(nt, BLOCK, SLAB), plane(nt, BLOCK, SLAB),
                plane(PAD + nt * BLOCK + 8, SLAB, dtype=F32),
                plane(PAD + nt * BLOCK + 8, SLAB, dtype=F32),
                plane(LANCZOS, nt * BLOCK, SLAB, dtype=F32),
                *[plane(groups, 8, 16, SLAB)] * 2,
                *[plane(nv, groups, 16, SLAB)] * 2,
                plane(groups, 16, SLAB, dtype=F32),
                *[plane(groups, 16, SLAB)] * 2,
                *[plane(nt, BLOCK, SLAB)] * 2,
                pltpu.SemaphoreType.DMA((2,)),
                pltpu.SemaphoreType.DMA((2,)),
                pltpu.SemaphoreType.DMA((8,)),
                pltpu.SemaphoreType.DMA((8,)),
            ],
            compiler_params=pltpu.CompilerParams(
                collective_id=0, has_side_effects=True, vmem_limit_bytes=48 * 2**20
            ),
        )(*args)

    placed = (
        P("visit", "tile", None),
        P("visit", "tile", None),
        P("visit", "tile"),
        P("visit"),
        P("visit", None),
        P(),
        P(),
        P("visit", None, None),
        P("visit", None),
        P("visit", None, "tile"),
    )
    return jax.shard_map(
        body,
        mesh=mesh,
        in_specs=placed,
        out_specs=(P("tile", None), P("tile", None)),
        check_vma=False,
    )
```

time: 406 us -> 67.3 us (0.17)
  other arithmetic: 169 us -> 0 us
  waiting for transfers between devices: 159 us -> 0 us
  Pallas kernels: 0 us -> 60.3 us
  starting transfers between devices: 47.7 us -> 0 us
  between operations: 15 us -> 1.35 us
  local copies, waits for them, and re-layouts: 12.7 us -> 5.38 us
    add x10 -> x0, other arithmetic: 162 us -> none  [the longest x1 89.2 us: match_psf(): result = result + weights[basis] * col_pass]
    ppermute x10 -> x0, waiting for transfers between devices: 83.6 us -> none  [the longest x6 81.1 us: passed_along(): return lax.ppermute(x, axis, pairs)]
    psum x1 -> x0, waiting for transfers between devices: 74.9 us -> none  [body(): total_numer, total_denom = lax.psum((numer, sky_ivar), 'visit')]
    pallas_call x0 -> x1, Pallas kernels: none -> 60.3 us  [body(): pl.pallas_call(functools.partial(kernel, nv, nt), out_shape=[jax.ShapeDty...]
    ppermute x10 -> x0, starting transfers between devices: 47.6 us -> none  [the longest x6 36.4 us: passed_along(): return lax.ppermute(x, axis, pairs)]
    slice x15 -> x0, local copies, waits for them, and re-layouts: 10.4 us -> none  [the longest x6 4.33 us: match_psf(): horizontal[basis, offset] * spread[:, offset:offset + columns]]
  transfers between devices with their start and end apart: 11 -> 0, of which waited for: 8 -> 0; matrix products, arithmetic and copies ran while one was open for 3% -> 0% of each run, Pallas kernels for 0% -> 0%
where the time goes in v1:
time: 67.3 us; the launch traced here: 67 us
  Pallas kernels  60.3 us (90%)
  local copies, waits for them, and re-layouts  5.38 us (8%)
  between operations  1.35 us (2%)
    pallas_call x1, Pallas kernels, body(): pl.pallas_call(functools.partial(kernel, nv, nt), out_shape=[jax.ShapeDty...  60.3 us
    unnamed x18, local copies, waits for them, and re-layouts  5.38 us

profile of v1, /device:TPU:1, one launch (start us, length us, event | category | flops | bytes accessed | tf_op | source)
XLA Modules:
  0.0 67.0 jit_solution(9486782149221963779)
XLA Ops:
  1.3 0.7 %copy.13.roww = f32[1,6,32]{2,1,0:T(8,128)S(1)} copy(f32[1,6,32]{2,0,1:T(1,128)} %param.19) | data formatting | bytes 1536 | tf_op args[9]
  2.0 0.0 copy-start.2
  2.0 0.0 copy-start.3
  2.0 0.0 copy-start.4
  2.0 0.0 copy-start.5
  2.0 0.0 copy-start.6
  2.0 1.0 %copy.12.colw = f32[1,6,4096]{2,1,0:T(8,128)S(1)} copy(f32[1,6,4096]{2,0,1:T(1,128)} %param.17) | data formatting | bytes 196608 | tf_op args[7]
  3.0 0.0 copy-done.2
  3.0 0.0 copy-done.3
  3.0 0.0 copy-done.4
  3.0 0.0 copy-done.5
  3.0 0.0 copy-done.6
  3.0 0.0 copy-start
  3.1 1.0 %copy-done = f32[1,32,4096]{2,1,0:T(8,128)S(1)} copy-done((f32[1,32,4096]{2,1,0:T(8,128)S(1)}, f32[1,32,4096]{2,1,0:T(8,128)}, u32[]{:S(2)}) %copy-start) | copy-done | bytes 524312
  4.1 0.0 copy-start.1
  4.1 1.0 %copy-done.1 = f32[1,32,4096]{2,1,0:T(8,128)S(1)} copy-done((f32[1,32,4096]{2,1,0:T(8,128)S(1)}, f32[1,32,4096]{2,1,0:T(8,128)}, u32[]{:S(2)}) %copy-start.1) | copy-done | bytes 524312
  5.1 60.3 %shard_map.113 = (f32[32,4096]{1,0:T(8,128)S(1)}, f32[32,4096]{1,0:T(8,128)S(1)}) custom-call(f32[1,32,4096]{2,1,0:T(8,128)S(1)} %copy-done, f32[1,32,4096]{2,1,0:T(8,128)S(1)} %copy-done.1, s32[1,32]{1,0:T(1,128)S(1)} %copy-done.5, s32[1]{0:T(128)S(6)} %copy.16.shift, f32[1,5]{1,0:T(1,128)S(1)} %copy-done.6, f32[5,21]{1,0:T(8,128)S(1)} %copy-done.3, ...), custom_call_target="tpu_custom_call" | custom-call | tf_op jit(solution)/shard_map/pallas_call | solution.py:420
  65.4 0.8 %copy.17 = f32[32,4096]{1,0:T(8,128)} copy(f32[32,4096]{1,0:T(8,128)S(1)} %get-tuple-element.4) | data formatting | bytes 1048576
  66.2 0.8 %copy.18 = f32[32,4096]{1,0:T(8,128)} copy(f32[32,4096]{1,0:T(8,128)S(1)} %get-tuple-element.5) | data formatting | bytes 1048576
Async XLA Ops:
  2.0 1.0 %copy-start.2 = (s32[1,4096]{1,0:T(1,128)S(1)}, s32[1,4096]{1,0:T(1,128)}, u32[]{:S(2)}) copy-start(s32[1,4096]{1,0:T(1,128)} %coloff.1) | copy-start | bytes 49156
  2.0 1.0 %copy-start.3 = (f32[5,21]{1,0:T(8,128)S(1)}, f32[5,21]{1,0:T(8,128)}, u32[]{:S(2)}) copy-start(f32[5,21]{1,0:T(8,128)} %vert.1) | copy-start | bytes 1264
  2.0 1.1 %copy-start.4 = (f32[5,21]{1,0:T(8,128)S(1)}, f32[5,21]{1,0:T(8,128)}, u32[]{:S(2)}) copy-start(f32[5,21]{1,0:T(8,128)} %horiz.1) | copy-start | bytes 1264
  2.0 1.1 %copy-start.5 = (s32[1,32]{1,0:T(1,128)S(1)}, s32[1,32]{1,0:T(1,128)}, u32[]{:S(2)}) copy-start(s32[1,32]{1,0:T(1,128)} %mask.1) | copy-start | bytes 388
  2.0 1.1 %copy-start.6 = (f32[1,5]{1,0:T(1,128)S(1)}, f32[1,5]{1,0:T(1,128)}, u32[]{:S(2)}) copy-start(f32[1,5]{1,0:T(1,128)} %coef.1) | copy-start | bytes 64
  3.0 1.0 %copy-start = (f32[1,32,4096]{2,1,0:T(8,128)S(1)}, f32[1,32,4096]{2,1,0:T(8,128)}, u32[]{:S(2)}) copy-start(f32[1,32,4096]{2,1,0:T(8,128)} %image.1) | copy-start | bytes 1572868
  4.1 1.0 %copy-start.1 = (f32[1,32,4096]{2,1,0:T(8,128)S(1)}, f32[1,32,4096]{2,1,0:T(8,128)}, u32[]{:S(2)}) copy-start(f32[1,32,4096]{2,1,0:T(8,128)} %variance.1) | copy-start | bytes 1572868

commit v2 on v1

v2 whole, which is shorter than its diff:
```python
import jax
import jax.numpy as jnp
from jax import lax
from jax.experimental import pallas as pl
from jax.experimental.pallas import tpu as pltpu
from jax.sharding import PartitionSpec as P

MESH = pl.DeviceIdType.MESH
F32 = jnp.float32
BF16 = jnp.bfloat16
TAPS = 21
RIM = 10
BASES = 5
LANCZOS = 6
BLOCK = 32
SLAB = 128
PAD = 520
NV = 8
NT = 32
ROWS = NT * BLOCK
WIDTH = NT * SLAB
PAIRS = NT // 2
CHUNKS = 4
SPAN = WIDTH // CHUNKS
HALF = WIDTH // 2


def split(x):
    high = x.astype(BF16)
    return high, (x - high.astype(F32)).astype(BF16)


def cols(j, n=SLAB):
    return pl.ds(pl.multiple_of(j * n, n), n)


def far_first(k, n):
    step = lax.div(k + 1, 2)
    return lax.rem(n // 2 + step * (1 - 2 * lax.rem(k, 2)), n)


def kernel(
    image_hbm, variance_hbm, mask, shift, coef, vert, horiz, colw, coloff, roww,
    f_nu, f_iv,
    image, variance,
    x_cat, v_mat, e_hi, e_lo, o_hi, o_lo, t_main_hi, t_main_lo, t_halo_hi, t_halo_lo,
    matched, factor, rw_mine, rw_quad, rw_all, s_iv, r_iv, s_cw, r_cw, ivf, cwf, wbi,
    nb_iv, nb_nu, c2_iv, c2_nu, total_iv, c3_iv, c3_nu,
    in_sem, halo_send, halo_recv, send_sem, recv_sem,
):
    v, t = lax.axis_index("visit"), lax.axis_index("tile")
    x, z = lax.div(t, 8), lax.rem(t, 8)
    y, core = lax.div(v, 2), lax.rem(v, 2)
    quad, place = lax.div(t, 4), lax.rem(t, 4)
    side = lax.div(t, NT // 2)
    to_self = (side == core) & (lax.rem(16 - 2 * z, 4) == y)

    get_image = pltpu.make_async_copy(image_hbm.at[0], image, in_sem.at[0])
    get_variance = pltpu.make_async_copy(variance_hbm.at[0], variance, in_sem.at[1])
    get_image.start()
    get_variance.start()

    barrier = pltpu.get_barrier_semaphore()

    def greet(v2, t2):
        pl.semaphore_signal(barrier, inc=1, device_id=(v2, t2), device_id_type=MESH)

    def greet_tile(k, c):
        greet(v, lax.rem(t + k, NT))
        return c

    def greet_visit(k, c):
        greet(lax.rem(v + k, NV), t)
        return c

    lax.fori_loop(1, NT, greet_tile, 0)
    lax.fori_loop(1, NV, greet_visit, 0)

    get_image.wait()

    def fill(j, c):
        x_cat[16:48, cols(j, 512)] = image[:, cols(j, 512)].astype(BF16)
        return c

    lax.fori_loop(0, WIDTH // 512, fill, 0)
    pl.semaphore_wait(barrier, (NT - 1) + (NV - 1))

    def halo(way, g):
        from_row, to_row, t2 = ((32, 0, lax.rem(t + 1, NT)), (16, 48, lax.rem(t + NT - 1, NT)))[way]
        return pltpu.make_async_remote_copy(
            src_ref=x_cat.at[pl.ds(from_row, 16), cols(g, SPAN)], dst_ref=x_cat.at[pl.ds(to_row, 16), cols(g, SPAN)],
            send_sem=halo_send.at[way, g], recv_sem=halo_recv.at[way, g],
            device_id=(v, t2), device_id_type=MESH)

    def start_halo(g, c):
        halo(0, g).start()
        halo(1, g).start()
        return c

    lax.fori_loop(0, CHUNKS, start_halo, 0)

    def fill_low(j, c):
        high = x_cat[16:48, cols(j, 512)]
        x_cat[112:144, cols(j, 512)] = high
        x_cat[64:96, cols(j, 512)] = (image[:, cols(j, 512)] - high.astype(F32)).astype(BF16)
        return c


    def send(source, target, at, v2, t2):
        pltpu.make_async_remote_copy(
            src_ref=source, dst_ref=target, send_sem=send_sem.at[at], recv_sem=recv_sem.at[at],
            device_id=(v2, t2), device_id_type=MESH).start()

    def arrived(ref, at):
        pltpu.make_async_copy(ref, ref, recv_sem.at[at]).wait()

    def left(ref, at):
        pltpu.make_async_copy(ref, ref, send_sem.at[at]).wait()

    rw_mine[...] = jnp.zeros_like(rw_mine)
    for q in range(4):
        for k in range(LANCZOS):
            rw_mine[k:k + 1, BLOCK * q:BLOCK * (q + 1)] = roww[k]
    lane = lax.broadcasted_iota(jnp.int32, (8, SLAB), 1)
    rw_mine[...] = jnp.where(lax.div(lane, BLOCK) == place, rw_mine[...], 0.0)
    for k in range(1, 4):
        send(rw_mine, rw_quad.at[place], 6, v, 4 * quad + lax.rem(place + k, 4))
    rw_quad[place] = rw_mine[...]

    flags = jnp.broadcast_to(mask[...].astype(F32), (BLOCK, BLOCK))
    same = lax.broadcasted_iota(jnp.int32, (BLOCK, BLOCK), 0) == lax.broadcasted_iota(jnp.int32, (BLOCK, BLOCK), 1)
    usable = jnp.sum(jnp.where(same, flags, 0.0), axis=1, keepdims=True)
    get_variance.wait()

    def weigh(j, c):
        s_iv[j] = (usable / variance[:, cols(j)]).astype(BF16)
        return c

    lax.fori_loop(0, NT, weigh, 0)

    def send_iv(k, c):
        x2 = lax.rem(x + far_first(lax.rem(k, 4), 4), 4)
        z2 = lax.rem(z + far_first(lax.div(k, 4), 8), 8)
        t2 = x2 * 8 + z2
        send(s_iv.at[t2], r_iv.at[t], 0, v, t2)
        return c

    lax.fori_loop(0, NT - 1, send_iv, 0)
    r_iv[t] = s_iv[t]
    lax.fori_loop(0, WIDTH // 512, fill_low, 0)

    r_at = lax.broadcasted_iota(jnp.int32, (BLOCK, 160), 0)
    q_at = lax.broadcasted_iota(jnp.int32, (BLOCK, 160), 1)
    q_row = jnp.where(q_at < 64, q_at - 16, jnp.where(q_at < 96, q_at - 64, q_at - 112))
    tap = q_row - r_at + RIM
    for b in range(BASES):
        value = jnp.zeros((BLOCK, 160), F32)
        for i in range(TAPS):
            value = jnp.where(tap == i, coef[0, b] * vert[b, i], value)
        high = value.astype(BF16).astype(F32)
        v_mat[BLOCK * b:BLOCK * (b + 1), :] = jnp.where(q_at < 96, high, value - high).astype(BF16)

    n_at = lax.broadcasted_iota(jnp.int32, (16, 256), 1)
    k_at = lax.broadcasted_iota(jnp.int32, (16, 256), 0)

    def band(d):
        values = [jnp.zeros((16, 256), F32) for _ in range(BASES)]
        for i in range(TAPS):
            hit = d == i
            values = [jnp.where(hit, horiz[b, i], values[b]) for b in range(BASES)]
        return [split(value) for value in values]

    def build(c, carry):
        parts = band(16 * c + k_at - n_at + RIM)
        at = pl.ds(pl.multiple_of(16 * c, 16), 16)
        for b in range(BASES):
            t_main_hi[b, at, :], t_main_lo[b, at, :] = parts[b]
            t_halo_hi[b, at, :] = jnp.zeros((16, 256), BF16)
            t_halo_lo[b, at, :] = jnp.zeros((16, 256), BF16)
        return carry

    lax.fori_loop(0, 16, build, 0)
    for start, gap in ((112, -118), (128, 138)):
        parts = band(start + k_at - n_at + gap)
        for b in range(BASES):
            t_halo_hi[b, start:start + 16, :], t_halo_lo[b, start:start + 16, :] = parts[b]

    c_at = lax.broadcasted_iota(jnp.int32, (1, 512), 1)

    def weights(g, c):
        delta = coloff[0:1, cols(g, 512)] - (c_at + 512 * g)
        sums = [jnp.zeros((1, 512), F32) for _ in range(11)]
        for gap in range(-5, 1):
            hit = delta == gap
            for k in range(LANCZOS):
                sums[gap + k + 5] = sums[gap + k + 5] + jnp.where(hit, colw[k, :, cols(g, 512)], 0.0)
        for d in range(11):
            factor[d:d + 1, cols(g, 512)] = sums[d]
        return c

    lax.fori_loop(0, WIDTH // 512, weights, 0)

    for ref in (e_hi, e_lo):
        ref[:, PAIRS] = jnp.zeros((BASES, BLOCK, SLAB), BF16)
    for ref in (o_hi, o_lo):
        ref[:, 0] = jnp.zeros((BASES, BLOCK, SLAB), BF16)
    matched[:, 0:SLAB] = jnp.zeros((BLOCK, SLAB), F32)
    matched[:, SLAB + WIDTH:] = jnp.zeros((BLOCK, SLAB), F32)
    for ref in (ivf, cwf):
        ref[0:PAD, :] = jnp.zeros((PAD, SLAB), F32)
        ref[PAD + ROWS:, :] = jnp.zeros((8, SLAB), F32)

    arrived(rw_quad.at[pl.ds(0, 3)], 6)
    rw_all[quad] = rw_quad[0] + rw_quad[1] + rw_quad[2] + rw_quad[3]
    for k in range(1, 8):
        send(rw_all.at[quad], rw_all.at[quad], 7, v, 4 * lax.rem(quad + k, 8) + place)

    def vertical(g):
        for way in range(2):
            halo(way, g).wait_recv()

        @pl.when(t == 0)
        def _():
            x_cat[0:16, cols(g, SPAN)] = jnp.zeros((16, SPAN), BF16)

        @pl.when(t == NT - 1)
        def _():
            x_cat[48:64, cols(g, SPAN)] = jnp.zeros((16, SPAN), BF16)

        x_cat[96:112, cols(g, SPAN)] = x_cat[0:16, cols(g, SPAN)]
        x_cat[144:160, cols(g, SPAN)] = x_cat[48:64, cols(g, SPAN)]

        passed = jnp.dot(v_mat[...], x_cat[:, cols(g, SPAN)], preferred_element_type=F32)
        for i in range(4):
            j = 4 * g + i
            for b in range(BASES):
                high, low = split(passed[BLOCK * b:BLOCK * (b + 1), 256 * i:256 * (i + 1)])
                e_hi[b, j], o_hi[b, j + 1] = high[:, :SLAB], high[:, SLAB:]
                e_lo[b, j], o_lo[b, j + 1] = low[:, :SLAB], low[:, SLAB:]

    def horizontal(g):
        def part(ref, b, start):
            return ref[b, pl.ds(4 * g + start, 4)].reshape(4 * BLOCK, SLAB)

        total = jnp.zeros((4 * BLOCK, 256), F32)
        for b in range(BASES):
            main_hi = jnp.concatenate([part(e_hi, b, 0), part(o_hi, b, 1)], axis=1)
            main_lo = jnp.concatenate([part(e_lo, b, 0), part(o_lo, b, 1)], axis=1)
            halo_hi = jnp.concatenate([part(o_hi, b, 0), part(e_hi, b, 1)], axis=1)
            halo_lo = jnp.concatenate([part(o_lo, b, 0), part(e_lo, b, 1)], axis=1)
            for data, matrix in (
                (main_hi, t_main_hi), (main_lo, t_main_hi), (main_hi, t_main_lo),
                (halo_hi, t_halo_hi), (halo_lo, t_halo_hi), (halo_hi, t_halo_lo),
            ):
                total = total + jnp.dot(data, matrix[b], preferred_element_type=F32)
        for i in range(4):
            at = pl.ds(pl.multiple_of(SPAN * g + 256 * i + SLAB, SLAB), 256)
            matched[:, at] = total[BLOCK * i:BLOCK * (i + 1)]

    def interpolate(g):
        def step(i, c):
            j = 2 * g + i
            for r in range(2):
                window = matched[16 * r:16 * (r + 1), pl.ds(pl.multiple_of(512 * j, 512), 768)]
                total = jnp.zeros((16, 512), F32)
                for d in range(-5, 6):
                    moved = pltpu.roll(window, (-d) % 768, 1) if d else window
                    total = total + factor[d + 5:d + 6, cols(j, 512)] * moved[:, SLAB:SLAB + 512]
                total = total.astype(BF16)
                for q in range(4):
                    s_cw[4 * j + q, 16 * r:16 * (r + 1), :] = total[:, SLAB * q:SLAB * (q + 1)]
            return c

        lax.fori_loop(0, 2, step, 0)

    def send_cw(g):
        def step(k, c):
            t2 = 8 * g + lax.rem(z + far_first(k, 8), 8)

            @pl.when(t2 != t)
            def _():
                send(s_cw.at[t2], r_cw.at[t], 1, v, t2)

            return c

        lax.fori_loop(0, 8, step, 0)

    def chunk(s, c):
        @pl.when(s < CHUNKS)
        def _():
            vertical(s)

        @pl.when((s >= 1) & (s < CHUNKS + 1))
        def _():
            horizontal(s - 1)

        @pl.when(s >= 2)
        def _():
            interpolate(s - 2)
            send_cw(s - 2)

        return c

    lax.fori_loop(0, CHUNKS + 2, chunk, 0)
    r_cw[t] = s_cw[t]

    def unpack(ref, target):
        def step(j, c):
            target[pl.ds(pl.multiple_of(PAD + BLOCK * j, 8), BLOCK), :] = ref[j].astype(F32)
            return c

        lax.fori_loop(0, NT, step, 0)

    def share(ref, g, plane):
        plane = plane.astype(BF16)
        for q in range(4):
            z2 = 4 * lax.rem(g, 2) + q
            u2 = 2 * lax.rem(lax.div(g, 2) + 24 - z2 - x - z, 4)
            ref[z2, pl.ds(u2, 2)] = plane[BLOCK * q:BLOCK * (q + 1)].reshape(2, 16, SLAB)

    arrived(r_iv.at[pl.ds(0, NT - 1)], 0)
    arrived(rw_all.at[pl.ds(0, 7)], 7)
    unpack(r_iv, ivf)
    amount = shift[0]
    pick = lax.broadcasted_iota(jnp.int32, (16, LANCZOS * SLAB), 0)
    pick = lax.rem(pick, 8) == lax.div(lax.broadcasted_iota(jnp.int32, (16, LANCZOS * SLAB), 1), SLAB)
    pick = pick.astype(F32).astype(BF16)
    row_at = lax.broadcasted_iota(jnp.int32, (SLAB, SLAB), 0)

    def spread(g, c):
        whole = rw_all[g]
        high = whole.astype(BF16).astype(F32)
        joined = jnp.concatenate([high, whole - high], axis=0).astype(BF16)
        wide = lax.dot_general(joined, pick, (((0,), (0,)), ((), ())), preferred_element_type=F32)
        sky = ivf[pl.ds(SLAB * g + PAD - amount, SLAB), :]
        share(nb_iv, g, sky)
        for k in range(LANCZOS):
            inside = row_at + (SLAB * g + k - 2) < ROWS
            wbi[k, cols(g), :] = jnp.where(inside, wide[:, SLAB * k:SLAB * (k + 1)] * sky, 0.0)
        return c

    lax.fori_loop(0, 8, spread, 0)

    def scatter(source, target, at):
        def step(k, c):
            v2 = lax.rem(v + far_first(k, NV), NV)
            send(source.at[:, v2], target.at[v], at, v2, t)
            return c

        lax.fori_loop(0, NV - 1, step, 0)
        target[v] = source[:, v]

    def deliver(source, target, at):
        rows, columns = pl.ds(pl.multiple_of(16 * core, 16), 16), cols(t)

        def step(k, c):
            z2 = lax.rem(z + far_first(k, 8), 8)
            t2 = 8 * lax.rem(y + z2 + x + z, 4) + z2
            for gap in (2, 1, 3):
                send(source.at[z2], target.at[rows, columns], at, 2 * lax.rem(y + gap, 4) + side, t2)
            me = (side == core) & (t2 == t)

            @pl.when(jnp.logical_not(me))
            def _():
                send(source.at[z2], target.at[rows, columns], at, 2 * y + side, t2)

            @pl.when(me)
            def _():
                pltpu.make_async_copy(source.at[z2], target.at[rows, columns], recv_sem.at[at]).start()

            return c

        lax.fori_loop(0, 8, step, 0)

    def swap(target, at):
        mine = target.at[:, cols(core, HALF)]
        send(mine, mine, at, v + 1 - 2 * core, t)

    def summed(ref, i):
        total = ref[0, i].astype(F32)
        for u in range(1, NV):
            total = total + ref[u, i].astype(F32)
        return total

    scatter(nb_iv, c2_iv, 2)

    arrived(r_cw.at[pl.ds(0, NT - 1)], 1)
    unpack(r_cw, cwf)

    def warp(g, c):
        total = jnp.zeros((SLAB, SLAB), F32)
        for k in range(LANCZOS):
            total = total + wbi[k, cols(g), :] * cwf[pl.ds(SLAB * g + PAD + k - 2 - amount, SLAB), :]
        share(nb_nu, g, total)
        return c

    lax.fori_loop(0, 8, warp, 0)
    scatter(nb_nu, c2_nu, 3)

    arrived(c2_iv.at[pl.ds(0, NV - 1)], 2)

    def add_iv(i, c):
        total = summed(c2_iv, i)
        total_iv[i] = total
        c3_iv[i] = total.astype(BF16)
        return c

    lax.fori_loop(0, 8, add_iv, 0)
    deliver(c3_iv, f_iv, 4)

    arrived(c2_nu.at[pl.ds(0, NV - 1)], 3)

    def add_nu(i, c):
        c3_nu[i] = (summed(c2_nu, i) / jnp.maximum(total_iv[i], 1.0)).astype(BF16)
        return c

    lax.fori_loop(0, 8, add_nu, 0)
    deliver(c3_nu, f_nu, 5)

    arrived(f_iv.at[:, pl.ds(0, HALF)], 4)
    swap(f_iv, 8)
    arrived(f_nu.at[:, pl.ds(0, HALF)], 5)
    swap(f_nu, 9)

    def halo_left(g, c):
        halo(0, g).wait_send()
        halo(1, g).wait_send()
        return c

    lax.fori_loop(0, CHUNKS, halo_left, 0)
    left(rw_quad.at[pl.ds(0, 3)], 6)
    left(rw_all.at[pl.ds(0, 7)], 7)
    left(s_iv.at[pl.ds(0, NT - 1)], 0)
    left(s_cw.at[pl.ds(0, NT - 1)], 1)
    left(c2_iv.at[pl.ds(0, NV - 1)], 2)
    left(c2_nu.at[pl.ds(0, NV - 1)], 3)
    for c3, at in ((c3_iv, 4), (c3_nu, 5)):
        @pl.when(to_self)
        def _():
            left(c3.at[pl.ds(0, NT - 1)], at)

        @pl.when(jnp.logical_not(to_self))
        def _():
            left(c3, at)

    for target, at in ((f_iv, 8), (f_nu, 9)):
        left(target.at[:, pl.ds(0, HALF)], at)
        arrived(target.at[:, pl.ds(0, HALF)], at)


def solution(mesh):
    def body(image, variance, mask, shift, coef, vert, horiz, colw, coloff, roww):
        vmem = pl.BlockSpec(memory_space=pltpu.VMEM)
        smem = pl.BlockSpec(memory_space=pltpu.SMEM)
        hbm = pl.BlockSpec(memory_space=pltpu.HBM)

        def plane(*shape, dtype=BF16):
            return pltpu.VMEM(shape, dtype)

        coadd, weight_sum = pl.pallas_call(
            kernel,
            out_shape=[jax.ShapeDtypeStruct((BLOCK, WIDTH), BF16)] * 2,
            in_specs=[hbm, hbm, vmem, smem, smem, smem, smem, vmem, vmem, vmem],
            out_specs=[vmem, vmem],
            scratch_shapes=[
                *[plane(BLOCK, WIDTH, dtype=F32)] * 2,
                plane(160, WIDTH),
                plane(160, 160),
                *[plane(BASES, PAIRS + 1, BLOCK, SLAB)] * 4,
                *[plane(BASES, 256, 256)] * 4,
                plane(BLOCK, WIDTH + 2 * SLAB, dtype=F32),
                plane(16, WIDTH, dtype=F32),
                plane(8, SLAB, dtype=F32),
                plane(4, 8, SLAB, dtype=F32),
                plane(8, 8, SLAB, dtype=F32),
                *[plane(NT, BLOCK, SLAB)] * 4,
                *[plane(PAD + ROWS + 8, SLAB, dtype=F32)] * 2,
                plane(LANCZOS, ROWS, SLAB, dtype=F32),
                *[plane(8, NV, 16, SLAB)] * 2,
                *[plane(NV, 8, 16, SLAB)] * 2,
                plane(8, 16, SLAB, dtype=F32),
                *[plane(NT, 16, SLAB)] * 2,
                pltpu.SemaphoreType.DMA((2,)),
                pltpu.SemaphoreType.DMA((2, CHUNKS)),
                pltpu.SemaphoreType.DMA((2, CHUNKS)),
                pltpu.SemaphoreType.DMA((10,)),
                pltpu.SemaphoreType.DMA((10,)),
            ],
            compiler_params=pltpu.CompilerParams(
                collective_id=0, has_side_effects=True, vmem_limit_bytes=60 * 2**20
            ),
        )(image, variance, mask, shift, coef, vert, horiz,
          jnp.transpose(colw, (1, 0, 2)), coloff, jnp.transpose(roww, (1, 0, 2)))
        return coadd.astype(F32), weight_sum.astype(F32)

    placed = (
        P("visit", "tile", None),
        P("visit", "tile", None),
        P("visit", "tile"),
        P("visit"),
        P("visit", None),
        P(),
        P(),
        P("visit", None, None),
        P("visit", None),
        P("visit", None, "tile"),
    )
    return jax.shard_map(
        body,
        mesh=mesh,
        in_specs=placed,
        out_specs=(P("tile", None), P("tile", None)),
        check_vma=False,
    )
```

time: 67.3 us -> 53.1 us (0.79)
  Pallas kernels: 60.3 us -> 49 us
  local copies, waits for them, and re-layouts: 5.38 us -> 0.01 us
  other arithmetic: 0 us -> 2.65 us
    pallas_call x1, Pallas kernels: 60.3 us -> 49 us  [body(): pl.pallas_call(kernel, out_shape=[jax.ShapeDtypeStruct((BLOCK, WIDTH), BF...]
    unnamed x18 -> x2, local copies, waits for them, and re-layouts: 5.38 us -> 0.01 us
    convert_element_type x0 -> x2, other arithmetic: none -> 2.65 us  [body(): return (coadd.astype(F32), weight_sum.astype(F32))]
where the time goes in v2:
time: 53.1 us; the launch traced here: 53 us
  Pallas kernels  49 us (92%)
  other arithmetic  2.65 us (5%)
  between operations  1.3 us (2%)
    pallas_call x1, Pallas kernels, body(): pl.pallas_call(kernel, out_shape=[jax.ShapeDtypeStruct((BLOCK, WIDTH), BF...  49 us
    convert_element_type x2, other arithmetic, body(): return (coadd.astype(F32), weight_sum.astype(F32))  2.65 us

profile of v2, /device:TPU:1, one launch (start us, length us, event | category | flops | bytes accessed | tf_op | source)
XLA Modules:
  0.0 53.0 jit_solution(17334821518752440618)
XLA Ops:
  1.3 49.0 %shard_map.113 = (bf16[32,4096]{1,0:T(8,128)(2,1)}, bf16[32,4096]{1,0:T(8,128)(2,1)}) custom-call(f32[1,32,4096]{2,1,0:T(8,128)} %image_hbm.1, f32[1,32,4096]{2,1,0:T(8,128)} %variance_hbm.1, s32[1,32]{1,0:T(1,128)} %mask.1, s32[1]{0:T(128)S(6)} %copy.12.shift, f32[1,5]{1,0:T(1,128)} %coef.1, f32[5,21]{1,0:T(8,128)} %vert.1, f32[5,21]{1,0:T(8,128)} %horiz.1, ...), custom_call_target="tpu_custom_call" | custom-call | tf_op jit(solution)/shard_map/pallas_call | solution.py:460
  50.3 0.0 copy-start
  50.3 1.8 %convert_element_type.6 = f32[32,4096]{1,0:T(8,128)} convert(bf16[32,4096]{1,0:T(8,128)(2,1)} %get-tuple-element.4) | non-fusion elementwise | flops 131072 | bytes 786432 | tf_op jit(solution)/shard_map/convert_element_type | solution.py:494
  52.2 0.0 copy-done
  52.2 0.8 %convert_element_type.7 = f32[32,4096]{1,0:T(8,128)} convert(bf16[32,4096]{1,0:T(8,128)(2,1)S(1)} %copy-done) | non-fusion elementwise | flops 131072 | bytes 786432 | tf_op jit(solution)/shard_map/convert_element_type | solution.py:494
Async XLA Ops:
  50.3 1.8 %copy-start = (bf16[32,4096]{1,0:T(8,128)(2,1)S(1)}, bf16[32,4096]{1,0:T(8,128)(2,1)}, u32[]{:S(2)}) copy-start(bf16[32,4096]{1,0:T(8,128)(2,1)} %get-tuple-element.5) | copy-start | bytes 786436

commit v3 on v2

--- a/solution.py
+++ b/solution.py
@@ -34,14 +34,14 @@
     return pl.ds(pl.multiple_of(j * n, n), n)
 
 
-def far_first(k, n):
-    step = lax.div(k + 1, 2)
-    return lax.rem(n // 2 + step * (1 - 2 * lax.rem(k, 2)), n)
+def far_first(n):
+    return sorted(range(n), key=lambda gap: -min(gap, n - gap))
 
 
 def kernel(
-    image_hbm, variance_hbm, mask, shift, coef, vert, horiz, colw, coloff, roww,
-    f_nu, f_iv,
+    image_hbm, variance_hbm, mask_hbm, shift, coef_hbm, vert_hbm, horiz_hbm, colw_hbm, coloff_hbm, roww_hbm,
+    final,
+    mask, coef, vert, horiz, colw, coloff, roww,
     image, variance,
     x_cat, v_mat, e_hi, e_lo, o_hi, o_lo, t_main_hi, t_main_lo, t_halo_hi, t_halo_lo,
     matched, factor, rw_mine, rw_quad, rw_all, s_iv, r_iv, s_cw, r_cw, ivf, cwf, wbi,
@@ -49,6 +49,7 @@
     in_sem, halo_send, halo_recv, send_sem, recv_sem,
 ):
     v, t = lax.axis_index("visit"), lax.axis_index("tile")
+    f_nu, f_iv = final.at[pl.ds(0, BLOCK)], final.at[pl.ds(BLOCK, BLOCK)]
     x, z = lax.div(t, 8), lax.rem(t, 8)
     y, core = lax.div(v, 2), lax.rem(v, 2)
     quad, place = lax.div(t, 4), lax.rem(t, 4)
@@ -58,6 +59,14 @@
     get_image = pltpu.make_async_copy(image_hbm.at[0], image, in_sem.at[0])
     get_variance = pltpu.make_async_copy(variance_hbm.at[0], variance, in_sem.at[1])
     get_image.start()
+    small = [
+        pltpu.make_async_copy(source, target, in_sem.at[i + 2])
+        for i, (source, target) in enumerate((
+            (mask_hbm, mask), (roww_hbm, roww), (coef_hbm, coef), (vert_hbm, vert),
+            (horiz_hbm, horiz), (colw_hbm, colw), (coloff_hbm, coloff)))
+    ]
+    for get in small:
+        get.start()
     get_variance.start()
 
     barrier = pltpu.get_barrier_semaphore()
@@ -65,16 +74,17 @@
     def greet(v2, t2):
         pl.semaphore_signal(barrier, inc=1, device_id=(v2, t2), device_id_type=MESH)
 
-    def greet_tile(k, c):
-        greet(v, lax.rem(t + k, NT))
-        return c
-
-    def greet_visit(k, c):
-        greet(lax.rem(v + k, NV), t)
-        return c
-
-    lax.fori_loop(1, NT, greet_tile, 0)
-    lax.fori_loop(1, NV, greet_visit, 0)
+    x_at = [8 * lax.rem(x + gap, 4) for gap in range(4)]
+    z_at = [lax.rem(z + gap, 8) for gap in range(8)]
+    y_at = [2 * lax.rem(y + gap, 4) for gap in range(4)]
+    tiles = sorted(((dx, dz) for dx in range(4) for dz in range(8)), key=lambda gap: -min(gap[0], 4 - gap[0]) - min(gap[1], 8 - gap[1]))
+    for dx, dz in tiles[:-1]:
+        greet(v, x_at[dx] + z_at[dz])
+    other = 1 - core
+    for gap in (2, 1, 3):
+        greet(y_at[gap] + core, t)
+        greet(y_at[gap] + other, t)
+    greet(y_at[0] + other, t)
 
     get_image.wait()
 
@@ -117,6 +127,8 @@
     def left(ref, at):
         pltpu.make_async_copy(ref, ref, send_sem.at[at]).wait()
 
+    for get in small:
+        get.wait()
     rw_mine[...] = jnp.zeros_like(rw_mine)
     for q in range(4):
         for k in range(LANCZOS):
@@ -138,14 +150,9 @@
 
     lax.fori_loop(0, NT, weigh, 0)
 
-    def send_iv(k, c):
-        x2 = lax.rem(x + far_first(lax.rem(k, 4), 4), 4)
-        z2 = lax.rem(z + far_first(lax.div(k, 4), 8), 8)
-        t2 = x2 * 8 + z2
+    for dx, dz in tiles[:-1]:
+        t2 = x_at[dx] + z_at[dz]
         send(s_iv.at[t2], r_iv.at[t], 0, v, t2)
-        return c
-
-    lax.fori_loop(0, NT - 1, send_iv, 0)
     r_iv[t] = s_iv[t]
     lax.fori_loop(0, WIDTH // 512, fill_low, 0)
 
@@ -274,16 +281,13 @@
         lax.fori_loop(0, 2, step, 0)
 
     def send_cw(g):
-        def step(k, c):
-            t2 = 8 * g + lax.rem(z + far_first(k, 8), 8)
-
-            @pl.when(t2 != t)
-            def _():
-                send(s_cw.at[t2], r_cw.at[t], 1, v, t2)
-
-            return c
-
-        lax.fori_loop(0, 8, step, 0)
+        for dz in far_first(8)[:-1]:
+            t2 = 8 * g + z_at[dz]
+            send(s_cw.at[t2], r_cw.at[t], 1, v, t2)
+
+        @pl.when(g != x)
+        def _():
+            send(s_cw.at[8 * g + z], r_cw.at[t], 1, v, 8 * g + z)
 
     def chunk(s, c):
         @pl.when(s < CHUNKS)
@@ -342,35 +346,32 @@
     lax.fori_loop(0, 8, spread, 0)
 
     def scatter(source, target, at):
-        def step(k, c):
-            v2 = lax.rem(v + far_first(k, NV), NV)
-            send(source.at[:, v2], target.at[v], at, v2, t)
-            return c
-
-        lax.fori_loop(0, NV - 1, step, 0)
+        for gap in (2, 1, 3, 0):
+            for seat in (core, other) if gap else (other,):
+                v2 = y_at[gap] + seat
+                send(source.at[:, v2], target.at[v], at, v2, t)
         target[v] = source[:, v]
 
     def deliver(source, target, at):
         rows, columns = pl.ds(pl.multiple_of(16 * core, 16), 16), cols(t)
 
-        def step(k, c):
-            z2 = lax.rem(z + far_first(k, 8), 8)
+        for dz in far_first(8):
+            z2 = z_at[dz]
             t2 = 8 * lax.rem(y + z2 + x + z, 4) + z2
             for gap in (2, 1, 3):
-                send(source.at[z2], target.at[rows, columns], at, 2 * lax.rem(y + gap, 4) + side, t2)
-            me = (side == core) & (t2 == t)
-
-            @pl.when(jnp.logical_not(me))
-            def _():
-                send(source.at[z2], target.at[rows, columns], at, 2 * y + side, t2)
-
-            @pl.when(me)
-            def _():
-                pltpu.make_async_copy(source.at[z2], target.at[rows, columns], recv_sem.at[at]).start()
-
-            return c
-
-        lax.fori_loop(0, 8, step, 0)
+                send(source.at[z2], target.at[rows, columns], at, y_at[gap] + side, t2)
+            if dz:
+                send(source.at[z2], target.at[rows, columns], at, y_at[0] + side, t2)
+        t2 = 8 * lax.rem(y + 2 * z + x, 4) + z
+        me = (side == core) & (t2 == t)
+
+        @pl.when(jnp.logical_not(me))
+        def _():
+            send(source.at[z], target.at[rows, columns], at, y_at[0] + side, t2)
+
+        @pl.when(me)
+        def _():
+            pltpu.make_async_copy(source.at[z], target.at[rows, columns], recv_sem.at[at]).start()
 
     def swap(target, at):
         mine = target.at[:, cols(core, HALF)]
@@ -457,12 +458,19 @@
         def plane(*shape, dtype=BF16):
             return pltpu.VMEM(shape, dtype)
 
-        coadd, weight_sum = pl.pallas_call(
+        both = pl.pallas_call(
             kernel,
-            out_shape=[jax.ShapeDtypeStruct((BLOCK, WIDTH), BF16)] * 2,
-            in_specs=[hbm, hbm, vmem, smem, smem, smem, smem, vmem, vmem, vmem],
-            out_specs=[vmem, vmem],
+            out_shape=jax.ShapeDtypeStruct((2 * BLOCK, WIDTH), BF16),
+            in_specs=[hbm, hbm, hbm, smem, *[hbm] * 6],
+            out_specs=vmem,
             scratch_shapes=[
+                plane(1, BLOCK, dtype=jnp.int32),
+                pltpu.SMEM((1, BASES), F32),
+                pltpu.SMEM((BASES, TAPS), F32),
+                pltpu.SMEM((BASES, TAPS), F32),
+                plane(LANCZOS, 1, WIDTH, dtype=F32),
+                plane(1, WIDTH, dtype=jnp.int32),
+                plane(LANCZOS, 1, BLOCK, dtype=F32),
                 *[plane(BLOCK, WIDTH, dtype=F32)] * 2,
                 plane(160, WIDTH),
                 plane(160, 160),
@@ -480,7 +488,7 @@
                 *[plane(NV, 8, 16, SLAB)] * 2,
                 plane(8, 16, SLAB, dtype=F32),
                 *[plane(NT, 16, SLAB)] * 2,
-                pltpu.SemaphoreType.DMA((2,)),
+                pltpu.SemaphoreType.DMA((9,)),
                 pltpu.SemaphoreType.DMA((2, CHUNKS)),
                 pltpu.SemaphoreType.DMA((2, CHUNKS)),
                 pltpu.SemaphoreType.DMA((10,)),
@@ -491,7 +499,8 @@
             ),
         )(image, variance, mask, shift, coef, vert, horiz,
           jnp.transpose(colw, (1, 0, 2)), coloff, jnp.transpose(roww, (1, 0, 2)))
-        return coadd.astype(F32), weight_sum.astype(F32)
+        both = both.astype(F32)
+        return both[:BLOCK], both[BLOCK:]
 
     placed = (
         P("visit", "tile", None),

time: 53.1 us -> 50.2 us (0.945)
  other arithmetic: 2.65 us -> 0 us
  Pallas kernels: 49 us -> 46.8 us
  local copies, waits for them, and re-layouts: 0.01 us -> 2.07 us
    convert_element_type x2 -> x0, other arithmetic: 2.65 us -> none  [body(): return (coadd.astype(F32), weight_sum.astype(F32))]
    pallas_call x1, Pallas kernels: 49 us -> 46.8 us  [body(): pl.pallas_call(kernel, out_shape=jax.ShapeDtypeStruct((2 * BLOCK, WIDTH),...]
    slice x0 -> x1, local copies, waits for them, and re-layouts: none -> 2.07 us  [body(): return (both[:BLOCK], both[BLOCK:])]
where the time goes in v3:
time: 50.2 us; the launch traced here: 50.1 us
  Pallas kernels  46.8 us (93%)
  local copies, waits for them, and re-layouts  2.07 us (4%)
  between operations  1.29 us (3%)
    pallas_call x1, Pallas kernels, body(): pl.pallas_call(kernel, out_shape=jax.ShapeDtypeStruct((2 * BLOCK, WIDTH),...  46.8 us
    slice x1, local copies, waits for them, and re-layouts, body(): return (both[:BLOCK], both[BLOCK:])  2.07 us

profile of v3, /device:TPU:1, one launch (start us, length us, event | category | flops | bytes accessed | tf_op | source)
XLA Modules:
  0.0 50.1 jit_solution(1230359035340671173)
XLA Ops:
  1.3 46.8 %shard_map.113 = bf16[64,4096]{1,0:T(8,128)(2,1)} custom-call(f32[1,32,4096]{2,1,0:T(8,128)} %image_hbm.1, f32[1,32,4096]{2,1,0:T(8,128)} %variance_hbm.1, s32[1,32]{1,0:T(1,128)} %mask_hbm.1, s32[1]{0:T(128)S(6)} %copy.12.shift, f32[1,5]{1,0:T(1,128)} %coef_hbm.1, f32[5,21]{1,0:T(8,128)} %vert_hbm.1, f32[5,21]{1,0:T(8,128)} %horiz_hbm.1, ...), custom_call_target="tpu_custom_call" | custom-call | tf_op jit(solution)/shard_map/pallas_call | solution.py:461
  48.0 2.1 %fusion = (f32[32,4096]{1,0:T(8,128)}, f32[32,4096]{1,0:T(8,128)}) fusion(bf16[64,4096]{1,0:T(8,128)(2,1)} %shard_map.113), kind=kLoop, calls=%fused_computation | loop fusion | bytes 2097152 | tf_op jit(solution)/shard_map/slice | solution.py:503

commit v4 on v3

--- a/solution.py
+++ b/solution.py
@@ -52,7 +52,6 @@
     f_nu, f_iv = final.at[pl.ds(0, BLOCK)], final.at[pl.ds(BLOCK, BLOCK)]
     x, z = lax.div(t, 8), lax.rem(t, 8)
     y, core = lax.div(v, 2), lax.rem(v, 2)
-    quad, place = lax.div(t, 4), lax.rem(t, 4)
     side = lax.div(t, NT // 2)
     to_self = (side == core) & (lax.rem(16 - 2 * z, 4) == y)
 
@@ -134,10 +133,10 @@
         for k in range(LANCZOS):
             rw_mine[k:k + 1, BLOCK * q:BLOCK * (q + 1)] = roww[k]
     lane = lax.broadcasted_iota(jnp.int32, (8, SLAB), 1)
-    rw_mine[...] = jnp.where(lax.div(lane, BLOCK) == place, rw_mine[...], 0.0)
-    for k in range(1, 4):
-        send(rw_mine, rw_quad.at[place], 6, v, 4 * quad + lax.rem(place + k, 4))
-    rw_quad[place] = rw_mine[...]
+    rw_mine[...] = jnp.where(lax.div(lane, BLOCK) == x, rw_mine[...], 0.0)
+    for dx in (2, 1, 3):
+        send(rw_mine, rw_quad.at[x], 6, v, x_at[dx] + z)
+    rw_quad[x] = rw_mine[...]
 
     flags = jnp.broadcast_to(mask[...].astype(F32), (BLOCK, BLOCK))
     same = lax.broadcasted_iota(jnp.int32, (BLOCK, BLOCK), 0) == lax.broadcasted_iota(jnp.int32, (BLOCK, BLOCK), 1)
@@ -218,9 +217,9 @@
         ref[PAD + ROWS:, :] = jnp.zeros((8, SLAB), F32)
 
     arrived(rw_quad.at[pl.ds(0, 3)], 6)
-    rw_all[quad] = rw_quad[0] + rw_quad[1] + rw_quad[2] + rw_quad[3]
-    for k in range(1, 8):
-        send(rw_all.at[quad], rw_all.at[quad], 7, v, 4 * lax.rem(quad + k, 8) + place)
+    rw_all[z] = rw_quad[0] + rw_quad[1] + rw_quad[2] + rw_quad[3]
+    for dz in far_first(8)[:-1]:
+        send(rw_all.at[z], rw_all.at[z], 7, v, 8 * x + z_at[dz])
 
     def vertical(g):
         for way in range(2):
@@ -315,12 +314,12 @@
 
         lax.fori_loop(0, NT, step, 0)
 
-    def share(ref, g, plane):
-        plane = plane.astype(BF16)
-        for q in range(4):
-            z2 = 4 * lax.rem(g, 2) + q
-            u2 = 2 * lax.rem(lax.div(g, 2) + 24 - z2 - x - z, 4)
-            ref[z2, pl.ds(u2, 2)] = plane[BLOCK * q:BLOCK * (q + 1)].reshape(2, 16, SLAB)
+    def share(ref, x2, z2, plane):
+        u2 = 2 * lax.rem(x2 + 24 - z2 - x - z, 4)
+        ref[z2, pl.ds(u2, 2)] = plane.astype(BF16).reshape(2, 16, SLAB)
+
+    def rows_of(x2, z2):
+        return 8 * BLOCK * x2 + pl.multiple_of(BLOCK * z2, BLOCK)
 
     arrived(r_iv.at[pl.ds(0, NT - 1)], 0)
     arrived(rw_all.at[pl.ds(0, 7)], 7)
@@ -329,40 +328,48 @@
     pick = lax.broadcasted_iota(jnp.int32, (16, LANCZOS * SLAB), 0)
     pick = lax.rem(pick, 8) == lax.div(lax.broadcasted_iota(jnp.int32, (16, LANCZOS * SLAB), 1), SLAB)
     pick = pick.astype(F32).astype(BF16)
-    row_at = lax.broadcasted_iota(jnp.int32, (SLAB, SLAB), 0)
-
-    def spread(g, c):
-        whole = rw_all[g]
+    row_at = lax.broadcasted_iota(jnp.int32, (BLOCK, SLAB), 0)
+
+    def spread(z2, c):
+        whole = rw_all[z2]
         high = whole.astype(BF16).astype(F32)
         joined = jnp.concatenate([high, whole - high], axis=0).astype(BF16)
         wide = lax.dot_general(joined, pick, (((0,), (0,)), ((), ())), preferred_element_type=F32)
-        sky = ivf[pl.ds(SLAB * g + PAD - amount, SLAB), :]
-        share(nb_iv, g, sky)
-        for k in range(LANCZOS):
-            inside = row_at + (SLAB * g + k - 2) < ROWS
-            wbi[k, cols(g), :] = jnp.where(inside, wide[:, SLAB * k:SLAB * (k + 1)] * sky, 0.0)
+        for x2 in range(4):
+            start = rows_of(x2, z2)
+            sky = ivf[pl.ds(start + PAD - amount, BLOCK), :]
+            share(nb_iv, x2, z2, sky)
+            for k in range(LANCZOS):
+                inside = row_at + (start + k - 2) < ROWS
+                weight = wide[BLOCK * x2:BLOCK * (x2 + 1), SLAB * k:SLAB * (k + 1)]
+                wbi[k, pl.ds(start, BLOCK), :] = jnp.where(inside, weight * sky, 0.0)
         return c
 
     lax.fori_loop(0, 8, spread, 0)
 
-    def scatter(source, target, at):
+    first = 1 - lax.div(z, 4)
+
+    def half(h):
+        return pl.ds(4 * h, 4)
+
+    def scatter(source, target, at, h):
         for gap in (2, 1, 3, 0):
             for seat in (core, other) if gap else (other,):
                 v2 = y_at[gap] + seat
-                send(source.at[:, v2], target.at[v], at, v2, t)
-        target[v] = source[:, v]
-
-    def deliver(source, target, at):
+                send(source.at[half(h), v2], target.at[v, half(h)], at, v2, t)
+        target[v, half(h)] = source[half(h), v]
+
+    def deliver(source, target, at, h, own):
         rows, columns = pl.ds(pl.multiple_of(16 * core, 16), 16), cols(t)
-
-        for dz in far_first(8):
-            z2 = z_at[dz]
+        for turn in (2, 1, 3, 0) if own else (0, 1, 3, 2):
+            z2 = 4 * h + lax.rem(z + turn, 4)
             t2 = 8 * lax.rem(y + z2 + x + z, 4) + z2
             for gap in (2, 1, 3):
                 send(source.at[z2], target.at[rows, columns], at, y_at[gap] + side, t2)
-            if dz:
+            if turn or not own:
                 send(source.at[z2], target.at[rows, columns], at, y_at[0] + side, t2)
-        t2 = 8 * lax.rem(y + 2 * z + x, 4) + z
+        if not own:
+            return
         me = (side == core) & (t2 == t)
 
         @pl.when(jnp.logical_not(me))
@@ -383,22 +390,24 @@
             total = total + ref[u, i].astype(F32)
         return total
 
-    scatter(nb_iv, c2_iv, 2)
+    for h, at in ((first, 2), (1 - first, 10)):
+        scatter(nb_iv, c2_iv, at, h)
 
     arrived(r_cw.at[pl.ds(0, NT - 1)], 1)
     unpack(r_cw, cwf)
 
-    def warp(g, c):
-        total = jnp.zeros((SLAB, SLAB), F32)
-        for k in range(LANCZOS):
-            total = total + wbi[k, cols(g), :] * cwf[pl.ds(SLAB * g + PAD + k - 2 - amount, SLAB), :]
-        share(nb_nu, g, total)
-        return c
-
-    lax.fori_loop(0, 8, warp, 0)
-    scatter(nb_nu, c2_nu, 3)
-
-    arrived(c2_iv.at[pl.ds(0, NV - 1)], 2)
+    def warp(z2, c):
+        for x2 in range(4):
+            start = rows_of(x2, z2)
+            total = jnp.zeros((BLOCK, SLAB), F32)
+            for k in range(LANCZOS):
+                total = total + wbi[k, pl.ds(start, BLOCK), :] * cwf[pl.ds(start + PAD + k - 2 - amount, BLOCK), :]
+            share(nb_nu, x2, z2, total)
+        return c
+
+    for h, at in ((first, 3), (1 - first, 11)):
+        lax.fori_loop(4 * h, 4 * h + 4, warp, 0)
+        scatter(nb_nu, c2_nu, at, h)
 
     def add_iv(i, c):
         total = summed(c2_iv, i)
@@ -406,17 +415,19 @@
         c3_iv[i] = total.astype(BF16)
         return c
 
-    lax.fori_loop(0, 8, add_iv, 0)
-    deliver(c3_iv, f_iv, 4)
-
-    arrived(c2_nu.at[pl.ds(0, NV - 1)], 3)
+    for h, at, own in ((first, 2, False), (1 - first, 10, True)):
+        arrived(c2_iv.at[pl.ds(0, NV - 1), half(0)], at)
+        lax.fori_loop(4 * h, 4 * h + 4, add_iv, 0)
+        deliver(c3_iv, f_iv, 4, h, own)
 
     def add_nu(i, c):
         c3_nu[i] = (summed(c2_nu, i) / jnp.maximum(total_iv[i], 1.0)).astype(BF16)
         return c
 
-    lax.fori_loop(0, 8, add_nu, 0)
-    deliver(c3_nu, f_nu, 5)
+    for h, at, own in ((first, 3, False), (1 - first, 11, True)):
+        arrived(c2_nu.at[pl.ds(0, NV - 1), half(0)], at)
+        lax.fori_loop(4 * h, 4 * h + 4, add_nu, 0)
+        deliver(c3_nu, f_nu, 5, h, own)
 
     arrived(f_iv.at[:, pl.ds(0, HALF)], 4)
     swap(f_iv, 8)
@@ -433,8 +444,8 @@
     left(rw_all.at[pl.ds(0, 7)], 7)
     left(s_iv.at[pl.ds(0, NT - 1)], 0)
     left(s_cw.at[pl.ds(0, NT - 1)], 1)
-    left(c2_iv.at[pl.ds(0, NV - 1)], 2)
-    left(c2_nu.at[pl.ds(0, NV - 1)], 3)
+    for target, at in ((c2_iv, 2), (c2_iv, 10), (c2_nu, 3), (c2_nu, 11)):
+        left(target.at[pl.ds(0, NV - 1), half(0)], at)
     for c3, at in ((c3_iv, 4), (c3_nu, 5)):
         @pl.when(to_self)
         def _():
@@ -457,6 +468,9 @@
 
         def plane(*shape, dtype=BF16):
             return pltpu.VMEM(shape, dtype)
+
+        def keep(array):
+            return pltpu.with_memory_space_constraint(array, pltpu.HBM)
 
         both = pl.pallas_call(
             kernel,
@@ -491,14 +505,14 @@
                 pltpu.SemaphoreType.DMA((9,)),
                 pltpu.SemaphoreType.DMA((2, CHUNKS)),
                 pltpu.SemaphoreType.DMA((2, CHUNKS)),
-                pltpu.SemaphoreType.DMA((10,)),
-                pltpu.SemaphoreType.DMA((10,)),
+                pltpu.SemaphoreType.DMA((12,)),
+                pltpu.SemaphoreType.DMA((12,)),
             ],
             compiler_params=pltpu.CompilerParams(
-                collective_id=0, has_side_effects=True, vmem_limit_bytes=60 * 2**20
+                collective_id=0, has_side_effects=True, vmem_limit_bytes=48 * 2**20
             ),
-        )(image, variance, mask, shift, coef, vert, horiz,
-          jnp.transpose(colw, (1, 0, 2)), coloff, jnp.transpose(roww, (1, 0, 2)))
+        )(keep(image), keep(variance), keep(mask), shift, keep(coef), keep(vert), keep(horiz),
+          keep(jnp.transpose(colw, (1, 0, 2))), keep(coloff), keep(jnp.transpose(roww, (1, 0, 2))))
         both = both.astype(F32)
         return both[:BLOCK], both[BLOCK:]
 

time: 50.2 us -> 45.8 us (0.912)
  Pallas kernels: 46.8 us -> 43.4 us
  local copies, waits for them, and re-layouts: 2.07 us -> 1.04 us
    pallas_call x1, Pallas kernels: 46.8 us -> 43.4 us  [body(): pl.pallas_call(kernel, out_shape=jax.ShapeDtypeStruct((2 * BLOCK, WIDTH),...]
    slice x1, local copies, waits for them, and re-layouts: 2.07 us -> 1.04 us  [body(): return (both[:BLOCK], both[BLOCK:])]
where the time goes in v4:
time: 45.8 us; the launch traced here: 45.7 us
  Pallas kernels  43.4 us (95%)
  between operations  1.29 us (3%)
  local copies, waits for them, and re-layouts  1.04 us (2%)
    pallas_call x1, Pallas kernels, body(): pl.pallas_call(kernel, out_shape=jax.ShapeDtypeStruct((2 * BLOCK, WIDTH),...  43.4 us
    slice x1, local copies, waits for them, and re-layouts, body(): return (both[:BLOCK], both[BLOCK:])  1.04 us

profile of v4, /device:TPU:1, one launch (start us, length us, event | category | flops | bytes accessed | tf_op | source)
XLA Modules:
  0.0 45.7 jit_solution(12575493929901021054)
XLA Ops:
  1.3 43.4 %shard_map.113 = bf16[64,4096]{1,0:T(8,128)(2,1)S(1)} custom-call(f32[1,32,4096]{2,1,0:T(8,128)} %image_hbm.1, f32[1,32,4096]{2,1,0:T(8,128)} %variance_hbm.1, s32[1,32]{1,0:T(1,128)} %mask_hbm.1, s32[1]{0:T(128)S(6)} %copy.12.shift, f32[1,5]{1,0:T(1,128)} %coef_hbm.1, f32[5,21]{1,0:T(8,128)} %vert_hbm.1, f32[5,21]{1,0:T(8,128)} %horiz_hbm.1, ...), custom_call_target="tpu_custom_call" | custom-call | tf_op jit(solution)/shard_map/pallas_call | solution.py:475
  44.7 1.0 %fusion = (f32[32,4096]{1,0:T(8,128)}, f32[32,4096]{1,0:T(8,128)}) fusion(bf16[64,4096]{1,0:T(8,128)(2,1)S(1)} %shard_map.113), kind=kLoop, calls=%fused_computation | loop fusion | bytes 2097152 | tf_op jit(solution)/shard_map/slice | solution.py:517

commit v5 on v4

--- a/solution.py
+++ b/solution.py
@@ -23,6 +23,7 @@
 CHUNKS = 4
 SPAN = WIDTH // CHUNKS
 HALF = WIDTH // 2
+FOLD = SPAN * RIM // 16
 
 
 def split(x):
@@ -42,7 +43,7 @@
     image_hbm, variance_hbm, mask_hbm, shift, coef_hbm, vert_hbm, horiz_hbm, colw_hbm, coloff_hbm, roww_hbm,
     final,
     mask, coef, vert, horiz, colw, coloff, roww,
-    image, variance,
+    image, variance, folded, opened, h_send, h_recv,
     x_cat, v_mat, e_hi, e_lo, o_hi, o_lo, t_main_hi, t_main_lo, t_halo_hi, t_halo_lo,
     matched, factor, rw_mine, rw_quad, rw_all, s_iv, r_iv, s_cw, r_cw, ivf, cwf, wbi,
     nb_iv, nb_nu, c2_iv, c2_nu, total_iv, c3_iv, c3_nu,
@@ -87,19 +88,31 @@
 
     get_image.wait()
 
-    def fill(j, c):
-        x_cat[16:48, cols(j, 512)] = image[:, cols(j, 512)].astype(BF16)
-        return c
-
-    lax.fori_loop(0, WIDTH // 512, fill, 0)
+    def folds(row):
+        return (
+            (slice(row, row + 10), 0, slice(0, 10), 0, FOLD),
+            (slice(row, row + 6), FOLD, slice(10, 16), 0, 384),
+            (slice(row + 6, row + 10), FOLD, slice(10, 14), 384, 256),
+            (slice(row + 6, row + 8), FOLD + 256, slice(14, 16), 384, 128),
+            (slice(row + 8, row + 10), FOLD + 256, slice(14, 16), 512, 128),
+        )
+
+    def pack(g, c):
+        for way, row in ((0, BLOCK - RIM), (1, 0)):
+            for rows, start, to_rows, to_start, size in folds(row):
+                at = pl.ds(pl.multiple_of(SPAN * g + start, SLAB), size)
+                folded[to_rows, to_start:to_start + size] = image[rows, at]
+            h_send[way, g] = folded[...].astype(BF16)
+        return c
+
+    lax.fori_loop(0, CHUNKS, pack, 0)
     pl.semaphore_wait(barrier, (NT - 1) + (NV - 1))
 
     def halo(way, g):
-        from_row, to_row, t2 = ((32, 0, lax.rem(t + 1, NT)), (16, 48, lax.rem(t + NT - 1, NT)))[way]
         return pltpu.make_async_remote_copy(
-            src_ref=x_cat.at[pl.ds(from_row, 16), cols(g, SPAN)], dst_ref=x_cat.at[pl.ds(to_row, 16), cols(g, SPAN)],
+            src_ref=h_send.at[way, g], dst_ref=h_recv.at[way, g],
             send_sem=halo_send.at[way, g], recv_sem=halo_recv.at[way, g],
-            device_id=(v, t2), device_id_type=MESH)
+            device_id=(v, lax.rem(t + (1, NT - 1)[way], NT)), device_id_type=MESH)
 
     def start_halo(g, c):
         halo(0, g).start()
@@ -109,7 +122,8 @@
     lax.fori_loop(0, CHUNKS, start_halo, 0)
 
     def fill_low(j, c):
-        high = x_cat[16:48, cols(j, 512)]
+        high = image[:, cols(j, 512)].astype(BF16)
+        x_cat[16:48, cols(j, 512)] = high
         x_cat[112:144, cols(j, 512)] = high
         x_cat[64:96, cols(j, 512)] = (image[:, cols(j, 512)] - high.astype(F32)).astype(BF16)
         return c
@@ -225,16 +239,14 @@
         for way in range(2):
             halo(way, g).wait_recv()
 
-        @pl.when(t == 0)
-        def _():
-            x_cat[0:16, cols(g, SPAN)] = jnp.zeros((16, SPAN), BF16)
-
-        @pl.when(t == NT - 1)
-        def _():
-            x_cat[48:64, cols(g, SPAN)] = jnp.zeros((16, SPAN), BF16)
-
-        x_cat[96:112, cols(g, SPAN)] = x_cat[0:16, cols(g, SPAN)]
-        x_cat[144:160, cols(g, SPAN)] = x_cat[48:64, cols(g, SPAN)]
+        for way, row, present, first_row, second_row in ((0, 6, t > 0, 0, 96), (1, 0, t < NT - 1, 48, 144)):
+            folded[...] = h_recv[way, g].astype(F32)
+            opened[...] = jnp.zeros_like(opened)
+            for rows, start, from_rows, from_start, size in folds(row):
+                opened[rows, start:start + size] = folded[from_rows, from_start:from_start + size]
+            near = jnp.where(present, opened[...], 0.0).astype(BF16)
+            x_cat[first_row:first_row + 16, cols(g, SPAN)] = near
+            x_cat[second_row:second_row + 16, cols(g, SPAN)] = near
 
         passed = jnp.dot(v_mat[...], x_cat[:, cols(g, SPAN)], preferred_element_type=F32)
         for i in range(4):
@@ -486,6 +498,9 @@
                 plane(1, WIDTH, dtype=jnp.int32),
                 plane(LANCZOS, 1, BLOCK, dtype=F32),
                 *[plane(BLOCK, WIDTH, dtype=F32)] * 2,
+                plane(16, FOLD, dtype=F32),
+                plane(16, SPAN, dtype=F32),
+                *[plane(2, CHUNKS, 16, FOLD)] * 2,
                 plane(160, WIDTH),
                 plane(160, 160),
                 *[plane(BASES, PAIRS + 1, BLOCK, SLAB)] * 4,

time: 45.8 us -> 45.1 us (0.985)
  Pallas kernels: 43.4 us -> 42.6 us
    pallas_call x1, Pallas kernels: 43.4 us -> 42.6 us  [body(): pl.pallas_call(kernel, out_shape=jax.ShapeDtypeStruct((2 * BLOCK, WIDTH),...]
where the time goes in v5:
time: 45.1 us; the launch traced here: 44.9 us
  Pallas kernels  42.6 us (94%)
  between operations  1.29 us (3%)
  local copies, waits for them, and re-layouts  1.04 us (2%)
    pallas_call x1, Pallas kernels, body(): pl.pallas_call(kernel, out_shape=jax.ShapeDtypeStruct((2 * BLOCK, WIDTH),...  42.6 us
    slice x1, local copies, waits for them, and re-layouts, body(): return (both[:BLOCK], both[BLOCK:])  1.04 us

profile of v5, /device:TPU:1, one launch (start us, length us, event | category | flops | bytes accessed | tf_op | source)
XLA Modules:
  0.0 44.9 jit_solution(16525418936974061178)
XLA Ops:
  1.3 42.6 %shard_map.113 = bf16[64,4096]{1,0:T(8,128)(2,1)S(1)} custom-call(f32[1,32,4096]{2,1,0:T(8,128)} %image_hbm.1, f32[1,32,4096]{2,1,0:T(8,128)} %variance_hbm.1, s32[1,32]{1,0:T(1,128)} %mask_hbm.1, s32[1]{0:T(128)S(6)} %copy.12.shift, f32[1,5]{1,0:T(1,128)} %coef_hbm.1, f32[5,21]{1,0:T(8,128)} %vert_hbm.1, f32[5,21]{1,0:T(8,128)} %horiz_hbm.1, ...), custom_call_target="tpu_custom_call" | custom-call | tf_op jit(solution)/shard_map/pallas_call | solution.py:487
  43.9 1.0 %fusion = (f32[32,4096]{1,0:T(8,128)}, f32[32,4096]{1,0:T(8,128)}) fusion(bf16[64,4096]{1,0:T(8,128)(2,1)S(1)} %shard_map.113), kind=kLoop, calls=%fused_computation | loop fusion | bytes 2097152 | tf_op jit(solution)/shard_map/slice | solution.py:532

commit v6 on v5

--- a/solution.py
+++ b/solution.py
@@ -78,8 +78,12 @@
     z_at = [lax.rem(z + gap, 8) for gap in range(8)]
     y_at = [2 * lax.rem(y + gap, 4) for gap in range(4)]
     tiles = sorted(((dx, dz) for dx in range(4) for dz in range(8)), key=lambda gap: -min(gap[0], 4 - gap[0]) - min(gap[1], 8 - gap[1]))
-    for dx, dz in tiles[:-1]:
-        greet(v, x_at[dx] + z_at[dz])
+    for dz in far_first(8)[:-1]:
+        greet(v, 8 * x + z_at[dz])
+    for dx in (2, 1, 3):
+        greet(v, x_at[dx] + z)
+    for step in (1, NT - 1):
+        greet(v, lax.rem(t + step, NT))
     other = 1 - core
     for gap in (2, 1, 3):
         greet(y_at[gap] + core, t)
@@ -106,7 +110,7 @@
         return c
 
     lax.fori_loop(0, CHUNKS, pack, 0)
-    pl.semaphore_wait(barrier, (NT - 1) + (NV - 1))
+    pl.semaphore_wait(barrier, 7 + 3 + 2 + (NV - 1))
 
     def halo(way, g):
         return pltpu.make_async_remote_copy(
@@ -163,9 +167,12 @@
 
     lax.fori_loop(0, NT, weigh, 0)
 
-    for dx, dz in tiles[:-1]:
-        t2 = x_at[dx] + z_at[dz]
-        send(s_iv.at[t2], r_iv.at[t], 0, v, t2)
+    def send_iv(gaps):
+        for dx, dz in gaps:
+            t2 = x_at[dx] + z_at[dz]
+            send(s_iv.at[t2], r_iv.at[t], 0, v, t2)
+
+    send_iv([gap for gap in tiles[:-1] if gap[0] == 0])
     r_iv[t] = s_iv[t]
     lax.fori_loop(0, WIDTH // 512, fill_low, 0)
 
@@ -180,6 +187,12 @@
         high = value.astype(BF16).astype(F32)
         v_mat[BLOCK * b:BLOCK * (b + 1), :] = jnp.where(q_at < 96, high, value - high).astype(BF16)
 
+    arrived(rw_quad.at[pl.ds(0, 3)], 6)
+    send_iv([gap for gap in tiles if gap[0]])
+    rw_all[z] = rw_quad[0] + rw_quad[1] + rw_quad[2] + rw_quad[3]
+    for dz in far_first(8)[:-1]:
+        send(rw_all.at[z], rw_all.at[z], 7, v, 8 * x + z_at[dz])
+
     n_at = lax.broadcasted_iota(jnp.int32, (16, 256), 1)
     k_at = lax.broadcasted_iota(jnp.int32, (16, 256), 0)
 
@@ -229,11 +242,6 @@
     for ref in (ivf, cwf):
         ref[0:PAD, :] = jnp.zeros((PAD, SLAB), F32)
         ref[PAD + ROWS:, :] = jnp.zeros((8, SLAB), F32)
-
-    arrived(rw_quad.at[pl.ds(0, 3)], 6)
-    rw_all[z] = rw_quad[0] + rw_quad[1] + rw_quad[2] + rw_quad[3]
-    for dz in far_first(8)[:-1]:
-        send(rw_all.at[z], rw_all.at[z], 7, v, 8 * x + z_at[dz])
 
     def vertical(g):
         for way in range(2):
@@ -321,10 +329,10 @@
 
     def unpack(ref, target):
         def step(j, c):
-            target[pl.ds(pl.multiple_of(PAD + BLOCK * j, 8), BLOCK), :] = ref[j].astype(F32)
+            target[pl.ds(pl.multiple_of(PAD + 8 * BLOCK * j, 8), 8 * BLOCK), :] = ref[pl.ds(8 * j, 8)].reshape(8 * BLOCK, SLAB).astype(F32)
             return c
 
-        lax.fori_loop(0, NT, step, 0)
+        lax.fori_loop(0, NT // 8, step, 0)
 
     def share(ref, x2, z2, plane):
         u2 = 2 * lax.rem(x2 + 24 - z2 - x - z, 4)

time: 45.1 us -> 44.4 us (0.984)
  Pallas kernels: 42.6 us -> 42 us
    pallas_call x1, Pallas kernels: 42.6 us -> 42 us  [body(): pl.pallas_call(kernel, out_shape=jax.ShapeDtypeStruct((2 * BLOCK, WIDTH),...]
where the time goes in v6:
time: 44.4 us; the launch traced here: 44.3 us
  Pallas kernels  42 us (95%)
  between operations  1.29 us (3%)
  local copies, waits for them, and re-layouts  1.04 us (2%)
    pallas_call x1, Pallas kernels, body(): pl.pallas_call(kernel, out_shape=jax.ShapeDtypeStruct((2 * BLOCK, WIDTH),...  42 us
    slice x1, local copies, waits for them, and re-layouts, body(): return (both[:BLOCK], both[BLOCK:])  1.04 us

profile of v6, /device:TPU:1, one launch (start us, length us, event | category | flops | bytes accessed | tf_op | source)
XLA Modules:
  0.0 44.3 jit_solution(10150604862245804443)
XLA Ops:
  1.3 42.0 %shard_map.113 = bf16[64,4096]{1,0:T(8,128)(2,1)S(1)} custom-call(f32[1,32,4096]{2,1,0:T(8,128)} %image_hbm.1, f32[1,32,4096]{2,1,0:T(8,128)} %variance_hbm.1, s32[1,32]{1,0:T(1,128)} %mask_hbm.1, s32[1]{0:T(128)S(6)} %copy.12.shift, f32[1,5]{1,0:T(1,128)} %coef_hbm.1, f32[5,21]{1,0:T(8,128)} %vert_hbm.1, f32[5,21]{1,0:T(8,128)} %horiz_hbm.1, ...), custom_call_target="tpu_custom_call" | custom-call | tf_op jit(solution)/shard_map/pallas_call | solution.py:495
  43.3 1.0 %fusion = (f32[32,4096]{1,0:T(8,128)}, f32[32,4096]{1,0:T(8,128)}) fusion(bf16[64,4096]{1,0:T(8,128)(2,1)S(1)} %shard_map.113), kind=kLoop, calls=%fused_computation | loop fusion | bytes 2097152 | tf_op jit(solution)/shard_map/slice | solution.py:540

commit v7 on v6

--- a/solution.py
+++ b/solution.py
@@ -15,6 +15,7 @@
 BLOCK = 32
 SLAB = 128
 PAD = 520
+PART = 2
 NV = 8
 NT = 32
 ROWS = NT * BLOCK
@@ -367,22 +368,22 @@
 
     lax.fori_loop(0, 8, spread, 0)
 
-    first = 1 - lax.div(z, 4)
-
-    def half(h):
-        return pl.ds(4 * h, 4)
+    parts = [(lax.rem(lax.div(z, PART) + gap, 8 // PART), i, gap == 0) for i, gap in enumerate(far_first(8 // PART))]
+
+    def part(h):
+        return pl.ds(PART * h, PART)
 
     def scatter(source, target, at, h):
         for gap in (2, 1, 3, 0):
             for seat in (core, other) if gap else (other,):
                 v2 = y_at[gap] + seat
-                send(source.at[half(h), v2], target.at[v, half(h)], at, v2, t)
-        target[v, half(h)] = source[half(h), v]
+                send(source.at[part(h), v2], target.at[v, part(h)], at, v2, t)
+        target[v, part(h)] = source[part(h), v]
 
     def deliver(source, target, at, h, own):
         rows, columns = pl.ds(pl.multiple_of(16 * core, 16), 16), cols(t)
-        for turn in (2, 1, 3, 0) if own else (0, 1, 3, 2):
-            z2 = 4 * h + lax.rem(z + turn, 4)
+        for turn in range(PART - 1, -1, -1):
+            z2 = PART * h + lax.rem(z + turn, PART)
             t2 = 8 * lax.rem(y + z2 + x + z, 4) + z2
             for gap in (2, 1, 3):
                 send(source.at[z2], target.at[rows, columns], at, y_at[gap] + side, t2)
@@ -410,8 +411,8 @@
             total = total + ref[u, i].astype(F32)
         return total
 
-    for h, at in ((first, 2), (1 - first, 10)):
-        scatter(nb_iv, c2_iv, at, h)
+    for h, i, own in parts:
+        scatter(nb_iv, c2_iv, 10 + i, h)
 
     arrived(r_cw.at[pl.ds(0, NT - 1)], 1)
     unpack(r_cw, cwf)
@@ -425,9 +426,9 @@
             share(nb_nu, x2, z2, total)
         return c
 
-    for h, at in ((first, 3), (1 - first, 11)):
-        lax.fori_loop(4 * h, 4 * h + 4, warp, 0)
-        scatter(nb_nu, c2_nu, at, h)
+    for h, i, own in parts:
+        lax.fori_loop(PART * h, PART * h + PART, warp, 0)
+        scatter(nb_nu, c2_nu, 18 + i, h)
 
     def add_iv(i, c):
         total = summed(c2_iv, i)
@@ -435,18 +436,18 @@
         c3_iv[i] = total.astype(BF16)
         return c
 
-    for h, at, own in ((first, 2, False), (1 - first, 10, True)):
-        arrived(c2_iv.at[pl.ds(0, NV - 1), half(0)], at)
-        lax.fori_loop(4 * h, 4 * h + 4, add_iv, 0)
+    for h, i, own in parts:
+        arrived(c2_iv.at[pl.ds(0, NV - 1), part(0)], 10 + i)
+        lax.fori_loop(PART * h, PART * h + PART, add_iv, 0)
         deliver(c3_iv, f_iv, 4, h, own)
 
     def add_nu(i, c):
         c3_nu[i] = (summed(c2_nu, i) / jnp.maximum(total_iv[i], 1.0)).astype(BF16)
         return c
 
-    for h, at, own in ((first, 3, False), (1 - first, 11, True)):
-        arrived(c2_nu.at[pl.ds(0, NV - 1), half(0)], at)
-        lax.fori_loop(4 * h, 4 * h + 4, add_nu, 0)
+    for h, i, own in parts:
+        arrived(c2_nu.at[pl.ds(0, NV - 1), part(0)], 18 + i)
+        lax.fori_loop(PART * h, PART * h + PART, add_nu, 0)
         deliver(c3_nu, f_nu, 5, h, own)
 
     arrived(f_iv.at[:, pl.ds(0, HALF)], 4)
@@ -464,8 +465,9 @@
     left(rw_all.at[pl.ds(0, 7)], 7)
     left(s_iv.at[pl.ds(0, NT - 1)], 0)
     left(s_cw.at[pl.ds(0, NT - 1)], 1)
-    for target, at in ((c2_iv, 2), (c2_iv, 10), (c2_nu, 3), (c2_nu, 11)):
-        left(target.at[pl.ds(0, NV - 1), half(0)], at)
+    for h, i, own in parts:
+        left(c2_iv.at[pl.ds(0, NV - 1), part(0)], 10 + i)
+        left(c2_nu.at[pl.ds(0, NV - 1), part(0)], 18 + i)
     for c3, at in ((c3_iv, 4), (c3_nu, 5)):
         @pl.when(to_self)
         def _():
@@ -528,8 +530,8 @@
                 pltpu.SemaphoreType.DMA((9,)),
                 pltpu.SemaphoreType.DMA((2, CHUNKS)),
                 pltpu.SemaphoreType.DMA((2, CHUNKS)),
-                pltpu.SemaphoreType.DMA((12,)),
-                pltpu.SemaphoreType.DMA((12,)),
+                pltpu.SemaphoreType.DMA((26,)),
+                pltpu.SemaphoreType.DMA((26,)),
             ],
             compiler_params=pltpu.CompilerParams(
                 collective_id=0, has_side_effects=True, vmem_limit_bytes=48 * 2**20

time: 44.4 us -> 44.8 us (level)
  no operation moved by 1% of the time
where the time goes in v7:
time: 44.8 us; the launch traced here: 44.7 us
  Pallas kernels  42.4 us (95%)
  between operations  1.29 us (3%)
  local copies, waits for them, and re-layouts  1.04 us (2%)
    pallas_call x1, Pallas kernels, body(): pl.pallas_call(kernel, out_shape=jax.ShapeDtypeStruct((2 * BLOCK, WIDTH),...  42.4 us
    slice x1, local copies, waits for them, and re-layouts, body(): return (both[:BLOCK], both[BLOCK:])  1.04 us

profile of v7, /device:TPU:1, one launch (start us, length us, event | category | flops | bytes accessed | tf_op | source)
XLA Modules:
  0.0 44.7 jit_solution(15924422418715675900)
XLA Ops:
  1.3 42.4 %shard_map.113 = bf16[64,4096]{1,0:T(8,128)(2,1)S(1)} custom-call(f32[1,32,4096]{2,1,0:T(8,128)} %image_hbm.1, f32[1,32,4096]{2,1,0:T(8,128)} %variance_hbm.1, s32[1,32]{1,0:T(1,128)} %mask_hbm.1, s32[1]{0:T(128)S(6)} %copy.12.shift, f32[1,5]{1,0:T(1,128)} %coef_hbm.1, f32[5,21]{1,0:T(8,128)} %vert_hbm.1, f32[5,21]{1,0:T(8,128)} %horiz_hbm.1, ...), custom_call_target="tpu_custom_call" | custom-call | tf_op jit(solution)/shard_map/pallas_call | solution.py:497
  43.7 1.0 %fusion = (f32[32,4096]{1,0:T(8,128)}, f32[32,4096]{1,0:T(8,128)}) fusion(bf16[64,4096]{1,0:T(8,128)(2,1)S(1)} %shard_map.113), kind=kLoop, calls=%fused_computation | loop fusion | bytes 2097152 | tf_op jit(solution)/shard_map/slice | solution.py:542
